TPU v7x, 512 devices: a whole 4x8x8 slice. The times are simulated.
512 devices in a mesh: ctx: 64 (over z_lo, x, y), head: 8 (over z_hi, core).
Axes of the slice: x: 4, y: 8, z: 8 (z_hi: 4, z_lo: 2; z = z_hi * 2 + z_lo), core: 2. Of those that a mesh axis runs over, the one named last changes fastest.
Arguments:
- queries: bfloat16 [32768, 4096], P(('ctx', 'head')), may hold values from -6 to 6
- stacked_keys: bfloat16 [32768, 1024], P(('ctx', 'head')), may hold values from -6 to 6
- stacked_values: bfloat16 [32768, 1024], P(('ctx', 'head')), may hold values from -6 to 6
- output_gradient: bfloat16 [32768, 4096], P(('ctx', 'head')), may hold values from -6 to 6
- doc_ids: int32 [32768], P('ctx'), may hold values from 0 to 127, never falling along the last dimension, each value on 1 to 1024 neighbouring positions
Outputs:
- attended: bfloat16 [32768, 4096], P(('ctx', 'head'))
- query_grad: bfloat16 [32768, 4096], P(('ctx', 'head'))
- key_grad: bfloat16 [32768, 1024], P(('ctx', 'head'))
- value_grad: bfloat16 [32768, 1024], P(('ctx', 'head'))
Inputs may be any that keep to these rules, and one draw needn't show every extreme that they name: `doc_ids`: document ids never fall along the sequence; each document has 1 to 1024 tokens and one has exactly 1024.
All inputs are finite; a program needn't handle non-finite values.
Results may differ from a plain program's by a relative error of at most 0.012.
The roundings to bfloat16 on the way count: a program that leaves them out, or rounds other values in their place, can miss the bound.
Values may be sent and summed in bfloat16 or wider, within the bound.
A program may use at most 64 MiB of HBM per device.

v0:
```python
import math

import jax
import jax.numpy as jnp
from jax import lax
from jax.sharding import PartitionSpec as P

HEAD_SIZE = 128
REACH = 2


def shifted(value, axis, steps):
    count = lax.axis_size(axis)
    initial, last = (max(0, -steps), min(count, count - steps))
    return lax.ppermute(value, axis, [(source, source + steps) for source in range(initial, last)])


def dot_rows(former, latter):
    return lax.dot_general(
        former, latter, (((0,), (0,)), ((), ())), preferred_element_type=jnp.float32
    )


def dot_last(former, latter):
    return lax.dot_general(
        former, latter, (((1,), (1,)), ((), ())), preferred_element_type=jnp.float32
    )


def masked_scores(query_tile, key_block, query_docs, key_docs, query_positions, key_positions):
    scores = dot_last(query_tile, key_block) * (1.0 / math.sqrt(HEAD_SIZE))
    allowed = (query_docs[:, None] == key_docs[None, :]) & (
        key_positions[None, :] <= query_positions[:, None]
    )
    return jnp.where(allowed, scores, -jnp.inf)


def score_grads(attention_probs, output_grad_block, value_block, dout_dot):
    dout_values = dot_last(output_grad_block, value_block)
    return (attention_probs.astype(jnp.float32) * (dout_values - dout_dot[:, None])).astype(
        jnp.bfloat16
    )


def by_heads(matrix, head_count):
    return matrix.reshape(matrix.shape[0], head_count, HEAD_SIZE).transpose(1, 0, 2)


def merge_heads(stacked):
    return stacked.transpose(1, 0, 2).reshape(stacked.shape[1], stacked.shape[0] * HEAD_SIZE)


def fold_groups(stacked, key_heads):
    grouped = stacked.reshape(
        key_heads, stacked.shape[0] // key_heads, stacked.shape[1], HEAD_SIZE
    ).sum(axis=1)
    return grouped.transpose(1, 0, 2).reshape(stacked.shape[1], key_heads * HEAD_SIZE)


def on_device(queries, stacked_keys, stacked_values, output_gradient, doc_ids):
    queries_here, keys_here, values_here, dout_here = (
        lax.all_to_all(queries, "head", split_axis=1, concat_axis=0, tiled=True),
        lax.all_to_all(stacked_keys, "head", split_axis=1, concat_axis=0, tiled=True),
        lax.all_to_all(stacked_values, "head", split_axis=1, concat_axis=0, tiled=True),
        lax.all_to_all(output_gradient, "head", split_axis=1, concat_axis=0, tiled=True),
    )
    row_count = queries_here.shape[0]
    query_heads = queries_here.shape[1] // HEAD_SIZE
    key_heads = keys_here.shape[1] // HEAD_SIZE
    group_width = query_heads // key_heads
    logit_scale = 1.0 / math.sqrt(HEAD_SIZE)
    shard_index = lax.axis_index("ctx")
    leading_row = shard_index * row_count
    own_positions = leading_row + jnp.arange(row_count, dtype=jnp.int32)
    received = [
        shifted((keys_here, values_here, doc_ids), "ctx", distance)
        for distance in range(1, REACH + 1)
    ]
    ordered = received[::-1] + [(keys_here, values_here, doc_ids)]
    window_keys = jnp.concatenate([triple[0] for triple in ordered], axis=0).reshape(
        -1, key_heads, HEAD_SIZE
    )
    window_values = jnp.concatenate([triple[1] for triple in ordered], axis=0).reshape(
        -1, key_heads, HEAD_SIZE
    )
    window_positions = (
        leading_row - REACH * row_count + jnp.arange((REACH + 1) * row_count, dtype=jnp.int32)
    )
    window_docs = jnp.where(
        window_positions >= 0, jnp.concatenate([triple[2] for triple in ordered], axis=0), -1
    )
    query_stack = by_heads(queries_here, query_heads)
    dout_stack = by_heads(dout_here, query_heads)
    head_to_key = jnp.arange(query_heads, dtype=jnp.int32) // group_width

    def window_head(inputs):
        query_tile, output_grad_block, key_index = inputs
        key_block = lax.dynamic_index_in_dim(window_keys, key_index, 1, keepdims=False)
        value_block = lax.dynamic_index_in_dim(window_values, key_index, 1, keepdims=False)
        scores = masked_scores(
            query_tile, key_block, doc_ids, window_docs, own_positions, window_positions
        )
        row_peak = jnp.max(scores, axis=1, keepdims=True)
        log_total = row_peak[:, 0] + jnp.log(jnp.sum(jnp.exp(scores - row_peak), axis=1))
        attention_probs = jnp.exp(scores - log_total[:, None]).astype(jnp.bfloat16)
        attended = jnp.dot(attention_probs, value_block, preferred_element_type=jnp.float32).astype(
            jnp.bfloat16
        )
        dout_dot = jnp.sum(
            attended.astype(jnp.float32) * output_grad_block.astype(jnp.float32), axis=1
        )
        score_gradient = score_grads(attention_probs, output_grad_block, value_block, dout_dot)
        query_grad = (
            logit_scale * jnp.dot(score_gradient, key_block, preferred_element_type=jnp.float32)
        ).astype(jnp.bfloat16)
        key_portion = logit_scale * dot_rows(score_gradient, query_tile)
        value_portion = dot_rows(attention_probs, output_grad_block)
        return (attended, query_grad, log_total, dout_dot, key_portion, value_portion)

    attended, query_grad, log_total, dout_dot, key_portion, value_portion = lax.map(
        window_head, (query_stack, dout_stack, head_to_key)
    )
    key_sum = fold_groups(key_portion, key_heads)
    value_sum = fold_groups(value_portion, key_heads)
    own_key = key_sum[REACH * row_count :]
    own_value = value_sum[REACH * row_count :]
    for distance in range(1, REACH + 1):
        segment_start = (REACH - distance) * row_count
        arrived = shifted(
            (
                key_sum[segment_start : segment_start + row_count],
                value_sum[segment_start : segment_start + row_count],
            ),
            "ctx",
            -distance,
        )
        own_key = own_key + arrived[0]
        own_value = own_value + arrived[1]
    results = (
        lax.all_to_all(merge_heads(attended), "head", split_axis=0, concat_axis=1, tiled=True),
        lax.all_to_all(merge_heads(query_grad), "head", split_axis=0, concat_axis=1, tiled=True),
        lax.all_to_all(
            own_key.astype(jnp.bfloat16), "head", split_axis=0, concat_axis=1, tiled=True
        ),
        lax.all_to_all(
            own_value.astype(jnp.bfloat16), "head", split_axis=0, concat_axis=1, tiled=True
        ),
    )
    return (results[0], results[1], results[2], results[3])


def solution(mesh):
    in_specs = (
        P(("ctx", "head"), None),
        P(("ctx", "head"), None),
        P(("ctx", "head"), None),
        P(("ctx", "head"), None),
        P("ctx"),
    )
    out_specs = (
        P(("ctx", "head"), None),
        P(("ctx", "head"), None),
        P(("ctx", "head"), None),
        P(("ctx", "head"), None),
    )
    return jax.shard_map(
        on_device, mesh=mesh, in_specs=in_specs, out_specs=out_specs, check_vma=False
    )
```

profile of v0, /device:TPU:62, one launch (start us, length us, event | category | flops | bytes accessed | tf_op | source)
XLA Modules:
  0.0 235.3 jit_solution(10694170069951014917)
XLA Ops:
  0.7 0.9 copy-done
  2.2 10.3 %all-to-all-start.1 = ((bf16[64,8,128]{2,0,1:T(8,128)(2,1)}), bf16[64,8,128]{2,0,1:T(8,128)(2,1)S(1)}, u32[]{:S(2)}, u32[]{:S(2)}) async-start(bf16[64,8,128]{2,0,1:T(8,128)(2,1)} %copy_bitcast_fusion.5), calls=%async_computation.1 | async-start | bytes 262144 | tf_op jit(solution)/shard_map/all_to_all | solution.py:63
  12.5 1.6 copy_bitcast_fusion.4
  14.1 8.4 %all-to-all-done.1 = bf16[64,8,128]{2,0,1:T(8,128)(2,1)S(1)} async-done(((bf16[64,8,128]{2,0,1:T(8,128)(2,1)}), bf16[64,8,128]{2,0,1:T(8,128)(2,1)S(1)}, u32[]{:S(2)}, u32[]{:S(2)}) %all-to-all-start.1) | async-done | bytes 131104 | tf_op jit(solution)/shard_map/all_to_all | solution.py:63
  22.5 3.4 %all-to-all-start.2 = ((bf16[64,8,128]{2,0,1:T(8,128)(2,1)}), bf16[64,8,128]{2,0,1:T(8,128)(2,1)S(1)}, u32[]{:S(2)}, u32[]{:S(2)}) async-start(bf16[64,8,128]{2,0,1:T(8,128)(2,1)} %copy_bitcast_fusion.4), calls=%async_computation.2 | async-start | bytes 262144 | tf_op jit(solution)/shard_map/all_to_all | solution.py:64
  25.9 1.9 copy.51
  27.7 7.6 %all-to-all-done.2 = bf16[64,8,128]{2,0,1:T(8,128)(2,1)S(1)} async-done(((bf16[64,8,128]{2,0,1:T(8,128)(2,1)}), bf16[64,8,128]{2,0,1:T(8,128)(2,1)S(1)}, u32[]{:S(2)}, u32[]{:S(2)}) %all-to-all-start.2) | async-done | bytes 131104 | tf_op jit(solution)/shard_map/all_to_all | solution.py:64
  35.4 3.5 %all-to-all-start = ((bf16[64,8,512]{2,0,1:T(8,128)(2,1)}), bf16[64,8,512]{2,0,1:T(8,128)(2,1)S(1)}, u32[]{:S(2)}, u32[]{:S(2)}) async-start(bf16[64,8,512]{2,0,1:T(8,128)(2,1)} %bitcast.124), calls=%async_computation | async-start | bytes 1048576 | tf_op jit(solution)/shard_map/all_to_all | solution.py:62
  39.7 17.2 %all-to-all-done = bf16[64,8,512]{2,0,1:T(8,128)(2,1)S(1)} async-done(((bf16[64,8,512]{2,0,1:T(8,128)(2,1)}), bf16[64,8,512]{2,0,1:T(8,128)(2,1)S(1)}, u32[]{:S(2)}, u32[]{:S(2)}) %all-to-all-start) | async-done | bytes 524320 | tf_op jit(solution)/shard_map/all_to_all | solution.py:62
  56.9 3.5 %all-to-all-start.3 = ((bf16[64,8,512]{2,0,1:T(8,128)(2,1)}), bf16[64,8,512]{2,0,1:T(8,128)(2,1)S(1)}, u32[]{:S(2)}, u32[]{:S(2)}) async-start(bf16[64,8,512]{2,0,1:T(8,128)(2,1)} %bitcast.123), calls=%async_computation.3 | async-start | bytes 1048576 | tf_op jit(solution)/shard_map/all_to_all | solution.py:65
  60.4 2.0 collective-permute-start.5
  62.4 4.5 %collective-permute-start.4 = (bf16[512,128]{1,0:T(8,128)(2,1)S(1)}, bf16[512,128]{1,0:T(8,128)(2,1)S(1)}, u32[]{:S(2)}, u32[]{:S(2)}) collective-permute-start(bf16[512,128]{1,0:T(8,128)(2,1)S(1)} %bitcast.177), channel_id=1, source_target_pairs={{0,16},{8,24},{16,32},{24,40},{32,48},{40,56},{48,64},{56,72},{64,... | collective-permute-start | bytes 393224 | tf_op jit(solution)/shard_map/ppermute | solution.py:15
  66.9 3.5 %collective-permute-start.1 = (s32[512]{0:T(512)S(1)}, s32[512]{0:T(512)S(1)}, u32[]{:S(2)}, u32[]{:S(2)}) collective-permute-start(s32[512]{0:T(512)S(1)} %copy-done.3), channel_id=1, source_target_pairs={{0,8},{8,16},{16,24},{24,32},{32,40},{40,48},{48,56},{56,64},{64,7... | collective-permute-start | bytes 6152 | tf_op jit(solution)/shard_map/ppermute | solution.py:15
  70.4 4.8 %collective-permute-start = (s32[512]{0:T(512)S(1)}, s32[512]{0:T(512)S(1)}, u32[]{:S(2)}, u32[]{:S(2)}) collective-permute-start(s32[512]{0:T(512)S(1)} %copy-done.3), channel_id=1, source_target_pairs={{0,16},{8,24},{16,32},{24,40},{32,48},{40,56},{48,64},{56,72},{64,... | collective-permute-start | bytes 6152 | tf_op jit(solution)/shard_map/ppermute | solution.py:15
  75.3 1.5 collective-permute-done
  76.8 8.9 %collective-permute-start.3 = (bf16[512,128]{1,0:T(8,128)(2,1)S(1)}, bf16[512,128]{1,0:T(8,128)(2,1)S(1)}, u32[]{:S(2)}, u32[]{:S(2)}) collective-permute-start(bf16[512,128]{1,0:T(8,128)(2,1)S(1)} %bitcast.173), channel_id=1, source_target_pairs={{0,8},{8,16},{16,24},{24,32},{32,40},{40,48},{48,56},{56,64},{64,7... | collective-permute-start | bytes 393224 | tf_op jit(solution)/shard_map/ppermute | solution.py:15
  85.7 2.0 collective-permute-start.2
  87.8 2.2 collective-permute-done.3
  90.0 3.6 %collective-permute-done.2 = bf16[512,128]{1,0:T(8,128)(2,1)S(1)} collective-permute-done((bf16[512,128]{1,0:T(8,128)(2,1)S(1)}, bf16[512,128]{1,0:T(8,128)(2,1)S(1)}, u32[]{:S(2)}, u32[]{:S(2)}) %collective-permute-start.2) | collective-permute-done | bytes 131104 | tf_op jit(solution)/shard_map/ppermute | solution.py:15
  94.3 33.8 %while.18 = (s32[]{:T(128)}, bf16[4,512,128]{1,2,0:T(8,128)(2,1)}, bf16[4,512,128]{2,1,0:T(8,128)(2,1)}, f32[4,1536,128]{2,1,0:T(8,128)}, f32[4,1536,128]{2,1,0:...) while((s32[]{:T(128)}, bf16[4,512,128]{1,2,0:T(8,128)(2,1)}, ...), condition=%wide.region_4.5_spmd.clone, body=%wide.region_0.4_spmd.clone.sunk | while | flops 1219625984 | bytes 24821928 | solution.py:120
  94.3 0.9 fusion.67
  96.4 1.3 bitcast_dynamic-update-slice_fusion.2
  98.5 1.2 fusion.69
  99.7 1.5 fusion.70
  101.2 1.5 fusion.71
  102.8 0.9 fusion.67
  104.8 1.3 bitcast_dynamic-update-slice_fusion.2
  106.9 1.2 fusion.69
  108.1 1.5 fusion.70
  109.7 1.5 fusion.71
  113.3 1.3 bitcast_dynamic-update-slice_fusion.2
  115.4 1.2 fusion.69
  116.6 1.5 fusion.70
  118.1 1.5 fusion.71
  119.6 0.9 fusion.67
  121.7 1.3 bitcast_dynamic-update-slice_fusion.2
  123.8 1.2 fusion.69
  125.0 1.5 fusion.70
  126.5 1.5 fusion.71
  128.0 3.2 %reduce_sum.44 = f32[1536,128]{1,0:T(8,128)} reduce(f32[4,1536,128]{2,1,0:T(8,128)} %get-tuple-element.107, f32[]{:T(128)} %constant.62.clone.1), dimensions={0}, to_apply=%region_6.7 | reduce | flops 589824 | bytes 3932164 | tf_op jit(solution)/shard_map/reduce_sum | solution.py:56
  131.2 1.9 slice_bitcast_fusion.1
  133.1 2.0 collective-permute-start.8
  135.1 1.9 collective-permute-start.9
  137.1 1.1 reduce_sum.42
  138.2 1.1 slice_bitcast_fusion.4
  139.2 3.7 %collective-permute-start.6 = (f32[512,128]{1,0:T(8,128)S(1)}, f32[512,128]{1,0:T(8,128)S(1)}, u32[]{:S(2)}, u32[]{:S(2)}) collective-permute-start(f32[512,128]{1,0:T(8,128)S(1)} %get-tuple-element.210), channel_id=1, source_target_pairs={{8,0},{16,8},{24,16},{32,24},{40,32},{48,40},{56,48},{64,56},{72,6... | collective-permute-start | bytes 786440 | tf_op jit(solution)/shard_map/ppermute | solution.py:15
  142.9 6.6 %collective-permute-start.7 = (f32[512,128]{1,0:T(8,128)S(1)}, f32[512,128]{1,0:T(8,128)S(1)}, u32[]{:S(2)}, u32[]{:S(2)}) collective-permute-start(f32[512,128]{1,0:T(8,128)S(1)} %get-tuple-element.211), channel_id=1, source_target_pairs={{16,0},{24,8},{32,16},{40,24},{48,32},{56,40},{64,48},{72,56},{80,... | collective-permute-start | bytes 786440 | tf_op jit(solution)/shard_map/ppermute | solution.py:15
  149.5 2.1 collective-permute-done.8
  151.5 7.6 %collective-permute-done.9 = f32[512,128]{1,0:T(8,128)} collective-permute-done((f32[512,128]{1,0:T(8,128)}, f32[512,128]{1,0:T(8,128)}, u32[]{:S(2)}, u32[]{:S(2)}) %collective-permute-start.9) | collective-permute-done | bytes 262176 | tf_op jit(solution)/shard_map/ppermute | solution.py:15
  159.1 1.7 fusion.31
  160.8 7.1 %all-to-all-start.7 = ((bf16[8,64,128]{2,1,0:T(8,128)(2,1)}), bf16[8,64,128]{2,1,0:T(8,128)(2,1)S(1)}, u32[]{:S(2)}, u32[]{:S(2)}) async-start(bf16[8,64,128]{2,1,0:T(8,128)(2,1)} %bitcast.26), calls=%async_computation.7 | async-start | bytes 262144 | tf_op jit(solution)/shard_map/all_to_all | solution.py:145
  168.0 5.2 %collective-permute-done.7 = f32[512,128]{1,0:T(8,128)S(1)} collective-permute-done((f32[512,128]{1,0:T(8,128)S(1)}, f32[512,128]{1,0:T(8,128)S(1)}, u32[]{:S(2)}, u32[]{:S(2)}) %collective-permute-start.7) | collective-permute-done | bytes 262176 | tf_op jit(solution)/shard_map/ppermute | solution.py:15
  173.2 1.6 fusion.34
  174.8 2.6 %all-to-all-done.7 = bf16[8,64,128]{2,1,0:T(8,128)(2,1)S(1)} async-done(((bf16[8,64,128]{2,1,0:T(8,128)(2,1)}), bf16[8,64,128]{2,1,0:T(8,128)(2,1)S(1)}, u32[]{:S(2)}, u32[]{:S(2)}) %all-to-all-start.7) | async-done | bytes 131104 | tf_op jit(solution)/shard_map/all_to_all | solution.py:145
  177.4 4.2 %all-to-all-start.6 = ((bf16[8,64,128]{2,1,0:T(8,128)(2,1)}), bf16[8,64,128]{2,1,0:T(8,128)(2,1)S(1)}, u32[]{:S(2)}, u32[]{:S(2)}) async-start(bf16[8,64,128]{2,1,0:T(8,128)(2,1)} %bitcast.20), calls=%async_computation.6 | async-start | bytes 262144 | tf_op jit(solution)/shard_map/all_to_all | solution.py:142
  181.7 1.4 copy.30
  183.0 1.0 all_to_all.122
  184.0 9.7 %all-to-all-done.6 = bf16[8,64,128]{2,1,0:T(8,128)(2,1)S(1)} async-done(((bf16[8,64,128]{2,1,0:T(8,128)(2,1)}), bf16[8,64,128]{2,1,0:T(8,128)(2,1)S(1)}, u32[]{:S(2)}, u32[]{:S(2)}) %all-to-all-start.6) | async-done | bytes 131104 | tf_op jit(solution)/shard_map/all_to_all | solution.py:142
  193.7 3.5 %all-to-all-start.4 = ((bf16[8,64,512]{2,1,0:T(8,128)(2,1)}), bf16[8,64,512]{2,1,0:T(8,128)(2,1)S(1)}, u32[]{:S(2)}, u32[]{:S(2)}) async-start(bf16[8,64,512]{2,1,0:T(8,128)(2,1)} %all_to_all.122), calls=%async_computation.4 | async-start | bytes 1048576 | tf_op jit(solution)/shard_map/all_to_all | solution.py:140
  197.2 1.5 copy.32
  198.7 1.0 all_to_all.126
  199.7 15.8 %all-to-all-done.4 = bf16[8,64,512]{2,1,0:T(8,128)(2,1)S(1)} async-done(((bf16[8,64,512]{2,1,0:T(8,128)(2,1)}), bf16[8,64,512]{2,1,0:T(8,128)(2,1)S(1)}, u32[]{:S(2)}, u32[]{:S(2)}) %all-to-all-start.4) | async-done | bytes 524320 | tf_op jit(solution)/shard_map/all_to_all | solution.py:140
  215.5 3.5 %all-to-all-start.5 = ((bf16[8,64,512]{2,1,0:T(8,128)(2,1)}), bf16[8,64,512]{2,1,0:T(8,128)(2,1)S(1)}, u32[]{:S(2)}, u32[]{:S(2)}) async-start(bf16[8,64,512]{2,1,0:T(8,128)(2,1)} %all_to_all.126), calls=%async_computation.5 | async-start | bytes 1048576 | tf_op jit(solution)/shard_map/all_to_all | solution.py:141
  221.2 13.3 %all-to-all-done.5 = bf16[8,64,512]{2,1,0:T(8,128)(2,1)S(1)} async-done(((bf16[8,64,512]{2,1,0:T(8,128)(2,1)}), bf16[8,64,512]{2,1,0:T(8,128)(2,1)S(1)}, u32[]{:S(2)}, u32[]{:S(2)}) %all-to-all-start.5) | async-done | bytes 524320 | tf_op jit(solution)/shard_map/all_to_all | solution.py:141
  (58 shorter events, 13.9 us)
Async XLA Ops:
  0.6 0.9 copy-start
  0.6 38.2 %copy-start.2 = (bf16[64,4096]{1,0:T(8,128)(2,1)S(1)}, bf16[64,4096]{1,0:T(8,128)(2,1)}, u32[]{:S(2)}) copy-start(bf16[64,4096]{1,0:T(8,128)(2,1)} %param.10) | copy-start | bytes 1572868
  1.5 65.4 %copy-start.3 = (s32[512]{0:T(512)S(1)}, s32[512]{0:T(512)}, u32[]{:S(2)}) copy-start(s32[512]{0:T(512)} %param.11) | copy-start | bytes 6148
  2.2 20.2 %all-to-all-start.1 = ((bf16[64,8,128]{2,0,1:T(8,128)(2,1)}), bf16[64,8,128]{2,0,1:T(8,128)(2,1)S(1)}, u32[]{:S(2)}, u32[]{:S(2)}) async-start(bf16[64,8,128]{2,0,1:T(8,128)(2,1)} %copy_bitcast_fusion.5), calls=%async_computation.1 | async-start | bytes 262144 | tf_op jit(solution)/shard_map/all_to_all | solution.py:63
  22.5 12.9 %all-to-all-start.2 = ((bf16[64,8,128]{2,0,1:T(8,128)(2,1)}), bf16[64,8,128]{2,0,1:T(8,128)(2,1)S(1)}, u32[]{:S(2)}, u32[]{:S(2)}) async-start(bf16[64,8,128]{2,0,1:T(8,128)(2,1)} %copy_bitcast_fusion.4), calls=%async_computation.2 | async-start | bytes 262144 | tf_op jit(solution)/shard_map/all_to_all | solution.py:64
  35.4 21.5 %all-to-all-start = ((bf16[64,8,512]{2,0,1:T(8,128)(2,1)}), bf16[64,8,512]{2,0,1:T(8,128)(2,1)S(1)}, u32[]{:S(2)}, u32[]{:S(2)}) async-start(bf16[64,8,512]{2,0,1:T(8,128)(2,1)} %bitcast.124), calls=%async_computation | async-start | bytes 1048576 | tf_op jit(solution)/shard_map/all_to_all | solution.py:62
  56.9 36.9 %all-to-all-start.3 = ((bf16[64,8,512]{2,0,1:T(8,128)(2,1)}), bf16[64,8,512]{2,0,1:T(8,128)(2,1)S(1)}, u32[]{:S(2)}, u32[]{:S(2)}) async-start(bf16[64,8,512]{2,0,1:T(8,128)(2,1)} %bitcast.123), calls=%async_computation.3 | async-start | bytes 1048576 | tf_op jit(solution)/shard_map/all_to_all | solution.py:65
  60.4 27.4 %collective-permute-start.5 = (bf16[512,128]{1,0:T(8,128)(2,1)S(1)}, bf16[512,128]{1,0:T(8,128)(2,1)S(1)}, u32[]{:S(2)}, u32[]{:S(2)}) collective-permute-start(bf16[512,128]{1,0:T(8,128)(2,1)S(1)} %bitcast.176), channel_id=1, source_target_pairs={{0,8},{8,16},{16,24},{24,32},{32,40},{40,48},{48,56},{56,64},{64,7... | collective-permute-start | bytes 393224 | tf_op jit(solution)/shard_map/ppermute | solution.py:15
  62.4 25.4 %collective-permute-start.4 = (bf16[512,128]{1,0:T(8,128)(2,1)S(1)}, bf16[512,128]{1,0:T(8,128)(2,1)S(1)}, u32[]{:S(2)}, u32[]{:S(2)}) collective-permute-start(bf16[512,128]{1,0:T(8,128)(2,1)S(1)} %bitcast.177), channel_id=1, source_target_pairs={{0,16},{8,24},{16,32},{24,40},{32,48},{40,56},{48,64},{56,72},{64,... | collective-permute-start | bytes 393224 | tf_op jit(solution)/shard_map/ppermute | solution.py:15
  66.9 8.4 %collective-permute-start.1 = (s32[512]{0:T(512)S(1)}, s32[512]{0:T(512)S(1)}, u32[]{:S(2)}, u32[]{:S(2)}) collective-permute-start(s32[512]{0:T(512)S(1)} %copy-done.3), channel_id=1, source_target_pairs={{0,8},{8,16},{16,24},{24,32},{32,40},{40,48},{48,56},{56,64},{64,7... | collective-permute-start | bytes 6152 | tf_op jit(solution)/shard_map/ppermute | solution.py:15
  70.4 6.4 %collective-permute-start = (s32[512]{0:T(512)S(1)}, s32[512]{0:T(512)S(1)}, u32[]{:S(2)}, u32[]{:S(2)}) collective-permute-start(s32[512]{0:T(512)S(1)} %copy-done.3), channel_id=1, source_target_pairs={{0,16},{8,24},{16,32},{24,40},{32,48},{40,56},{48,64},{56,72},{64,... | collective-permute-start | bytes 6152 | tf_op jit(solution)/shard_map/ppermute | solution.py:15
  76.8 13.2 %collective-permute-start.3 = (bf16[512,128]{1,0:T(8,128)(2,1)S(1)}, bf16[512,128]{1,0:T(8,128)(2,1)S(1)}, u32[]{:S(2)}, u32[]{:S(2)}) collective-permute-start(bf16[512,128]{1,0:T(8,128)(2,1)S(1)} %bitcast.173), channel_id=1, source_target_pairs={{0,8},{8,16},{16,24},{24,32},{32,40},{40,48},{48,56},{56,64},{64,7... | collective-permute-start | bytes 393224 | tf_op jit(solution)/shard_map/ppermute | solution.py:15
  85.7 7.9 %collective-permute-start.2 = (bf16[512,128]{1,0:T(8,128)(2,1)S(1)}, bf16[512,128]{1,0:T(8,128)(2,1)S(1)}, u32[]{:S(2)}, u32[]{:S(2)}) collective-permute-start(bf16[512,128]{1,0:T(8,128)(2,1)S(1)} %bitcast.174), channel_id=1, source_target_pairs={{0,16},{8,24},{16,32},{24,40},{32,48},{40,56},{48,64},{56,72},{64,... | collective-permute-start | bytes 393224 | tf_op jit(solution)/shard_map/ppermute | solution.py:15
  128.0 9.0 %copy-start.1 = (f32[4,1536,128]{2,1,0:T(8,128)S(1)}, f32[4,1536,128]{2,1,0:T(8,128)}, u32[]{:S(2)}) copy-start(f32[4,1536,128]{2,1,0:T(8,128)} %get-tuple-element.106) | copy-start | bytes 9437188
  133.1 18.4 %collective-permute-start.8 = (f32[512,128]{1,0:T(8,128)}, f32[512,128]{1,0:T(8,128)S(1)}, u32[]{:S(2)}, u32[]{:S(2)}) collective-permute-start(f32[512,128]{1,0:T(8,128)} %get-tuple-element.208), channel_id=1, source_target_pairs={{8,0},{16,8},{24,16},{32,24},{40,32},{48,40},{56,48},{64,56},{72,6... | collective-permute-start | bytes 786440 | tf_op jit(solution)/shard_map/ppermute | solution.py:15
  135.1 24.0 %collective-permute-start.9 = (f32[512,128]{1,0:T(8,128)}, f32[512,128]{1,0:T(8,128)}, u32[]{:S(2)}, u32[]{:S(2)}) collective-permute-start(f32[512,128]{1,0:T(8,128)} %get-tuple-element.209), channel_id=1, source_target_pairs={{16,0},{24,8},{32,16},{40,24},{48,32},{56,40},{64,48},{72,56},{80,... | collective-permute-start | bytes 786440 | tf_op jit(solution)/shard_map/ppermute | solution.py:15
  139.2 28.7 %collective-permute-start.6 = (f32[512,128]{1,0:T(8,128)S(1)}, f32[512,128]{1,0:T(8,128)S(1)}, u32[]{:S(2)}, u32[]{:S(2)}) collective-permute-start(f32[512,128]{1,0:T(8,128)S(1)} %get-tuple-element.210), channel_id=1, source_target_pairs={{8,0},{16,8},{24,16},{32,24},{40,32},{48,40},{56,48},{64,56},{72,6... | collective-permute-start | bytes 786440 | tf_op jit(solution)/shard_map/ppermute | solution.py:15
  142.9 30.3 %collective-permute-start.7 = (f32[512,128]{1,0:T(8,128)S(1)}, f32[512,128]{1,0:T(8,128)S(1)}, u32[]{:S(2)}, u32[]{:S(2)}) collective-permute-start(f32[512,128]{1,0:T(8,128)S(1)} %get-tuple-element.211), channel_id=1, source_target_pairs={{16,0},{24,8},{32,16},{40,24},{48,32},{56,40},{64,48},{72,56},{80,... | collective-permute-start | bytes 786440 | tf_op jit(solution)/shard_map/ppermute | solution.py:15
  160.8 16.6 %all-to-all-start.7 = ((bf16[8,64,128]{2,1,0:T(8,128)(2,1)}), bf16[8,64,128]{2,1,0:T(8,128)(2,1)S(1)}, u32[]{:S(2)}, u32[]{:S(2)}) async-start(bf16[8,64,128]{2,1,0:T(8,128)(2,1)} %bitcast.26), calls=%async_computation.7 | async-start | bytes 262144 | tf_op jit(solution)/shard_map/all_to_all | solution.py:145
  177.4 16.3 %all-to-all-start.6 = ((bf16[8,64,128]{2,1,0:T(8,128)(2,1)}), bf16[8,64,128]{2,1,0:T(8,128)(2,1)S(1)}, u32[]{:S(2)}, u32[]{:S(2)}) async-start(bf16[8,64,128]{2,1,0:T(8,128)(2,1)} %bitcast.20), calls=%async_computation.6 | async-start | bytes 262144 | tf_op jit(solution)/shard_map/all_to_all | solution.py:142
  193.7 21.8 %all-to-all-start.4 = ((bf16[8,64,512]{2,1,0:T(8,128)(2,1)}), bf16[8,64,512]{2,1,0:T(8,128)(2,1)S(1)}, u32[]{:S(2)}, u32[]{:S(2)}) async-start(bf16[8,64,512]{2,1,0:T(8,128)(2,1)} %all_to_all.122), calls=%async_computation.4 | async-start | bytes 1048576 | tf_op jit(solution)/shard_map/all_to_all | solution.py:140
  215.5 19.0 %all-to-all-start.5 = ((bf16[8,64,512]{2,1,0:T(8,128)(2,1)}), bf16[8,64,512]{2,1,0:T(8,128)(2,1)S(1)}, u32[]{:S(2)}, u32[]{:S(2)}) async-start(bf16[8,64,512]{2,1,0:T(8,128)(2,1)} %all_to_all.126), calls=%async_computation.5 | async-start | bytes 1048576 | tf_op jit(solution)/shard_map/all_to_all | solution.py:141
where the time goes:
time: 237 us; the launch traced here: 235 us
  waiting for transfers between devices  96.7 us (41%)
  starting transfers between devices  78.9 us (33%)
  matrix products  28.8 us (12%)
  local copies, waits for them, and re-layouts  17.3 us (7%)
  other arithmetic  12.6 us (5%)
    ppermute x10, starting transfers between devices, shifted(): lax.ppermute(value, axis, [(source, source + steps) for source in range(i...  39.9 us
    ppermute x10, waiting for transfers between devices, shifted(): lax.ppermute(value, axis, [(source, source + steps) for source in range(i...  22.1 us
    all_to_all x1, waiting for transfers between devices, on_device(): lax.all_to_all(queries, 'head', split_axis=1, concat_axis=0, tiled=True)  17.2 us
    all_to_all x1, waiting for transfers between devices, on_device(): lax.all_to_all(merge_heads(attended), 'head', split_axis=0, concat_axis=1...  15.8 us
    all_to_all x1, waiting for transfers between devices, on_device(): lax.all_to_all(merge_heads(query_grad), 'head', split_axis=0, concat_axis...  13.3 us
    dot_general x8, matrix products, dot_rows(): lax.dot_general(former, latter, (((0,), (0,)), ((), ())), preferred_eleme...  12.1 us
    all_to_all x1, starting transfers between devices, on_device(): lax.all_to_all(stacked_keys, 'head', split_axis=1, concat_axis=0, tiled=T...  10.3 us
    all_to_all x1, waiting for transfers between devices, on_device(): lax.all_to_all(own_key.astype(jnp.bfloat16), 'head', split_axis=0, concat...  9.7 us
  transfers between devices with their start and end apart: 18, of which 13 were waited for; matrix products, arithmetic and copies ran while one was open for 6% of the time, Pallas kernels for 0%

commit v1 on v0

v1 whole, which is shorter than its diff:
```python
import math

import jax
import jax.numpy as jnp
from jax import lax
from jax.experimental import pallas as pl
from jax.experimental.pallas import tpu as pltpu
from jax.sharding import PartitionSpec as P

D = 128
TOK = 64
SL = 128
BLK = 512
WIN = 1536
KEYS = 1152
GRP = 4
MESH = pl.DeviceIdType.MESH
SCALE = 1.0 / math.sqrt(D)
LOG2E = 1.4426950408889634


def nt(a, b):
    return lax.dot_general(a, b, (((1,), (1,)), ((), ())), preferred_element_type=jnp.float32)


def tn(a, b):
    return lax.dot_general(a, b, (((0,), (0,)), ((), ())), preferred_element_type=jnp.float32)


def kernel(
    q_ref, k_ref, v_ref, g_ref, doc_ref,
    att_ref, dq_ref, dk_ref, dv_ref,
    kv, qg, docw, startb, outb, acc, hsend, hrecv, osend,
    kv_send, kv_recv, qg_send, qg_recv, halo_send, halo_recv, doc_send, doc_recv, own_sem,
    out_send, out_recv, part_send, part_recv, grad_send, grad_recv,
):
    n_ctx = lax.axis_size("ctx")
    c = lax.axis_index("ctx")
    h = lax.axis_index("head")
    zh = h // 2
    core = lax.rem(h, 2)

    def head_dev(dz, dk):
        return lax.rem(zh + dz, 4) * 2 + lax.rem(core + dk, 2)

    def ctx_dev(dc):
        return lax.rem(c + dc + n_ctx, n_ctx)

    peers = [(0, 1), (1, 0), (1, 1), (3, 0), (3, 1), (2, 0), (2, 1)]

    own_row = pl.multiple_of(2 * BLK + h * TOK, TOK)
    col_q = pl.multiple_of(h * BLK, BLK)
    col_k = pl.multiple_of(h * D, D)
    tok_row = pl.multiple_of(core * TOK, TOK)
    for i, src in enumerate((k_ref, v_ref)):
        pltpu.make_async_copy(src.at[:, pl.ds(col_k, D)], kv.at[i, pl.ds(own_row, TOK)], kv_recv).start()
    for i, src in enumerate((q_ref, g_ref)):
        pltpu.make_async_copy(
            src.at[:, pl.ds(col_q, BLK)], qg.at[zh, i, pl.ds(tok_row, TOK)], qg_recv.at[zh]
        ).start()
    pltpu.make_async_copy(doc_ref, docw.at[2], own_sem).start()

    barrier = pltpu.get_barrier_semaphore()
    for dz, dk in peers:
        pl.semaphore_signal(barrier, inc=1, device_id=(c, head_dev(dz, dk)), device_id_type=MESH)
    for dc in (-2, -1, 1, 2):
        pl.semaphore_signal(barrier, inc=1, device_id=(ctx_dev(dc), h), device_id_type=MESH)
    pl.semaphore_wait(barrier, len(peers) + 4)

    for dz, dk in peers:
        p = head_dev(dz, dk)
        for i, src in enumerate((k_ref, v_ref)):
            pltpu.make_async_remote_copy(
                src_ref=src.at[:, pl.ds(pl.multiple_of(p * D, D), D)],
                dst_ref=kv.at[i, pl.ds(own_row, TOK)],
                send_sem=kv_send, recv_sem=kv_recv, device_id=(c, p), device_id_type=MESH,
            ).start()
    for dc in (1, 2):
        pltpu.make_async_remote_copy(
            src_ref=doc_ref, dst_ref=docw.at[2 - dc], send_sem=doc_send.at[dc - 1], recv_sem=doc_recv.at[dc - 1],
            device_id=(ctx_dev(dc), h), device_id_type=MESH,
        ).start()
    for dz, dk in peers:
        p = head_dev(dz, dk)
        for i, src in enumerate((q_ref, g_ref)):
            pltpu.make_async_remote_copy(
                src_ref=src.at[:, pl.ds(pl.multiple_of(p * BLK, BLK), BLK)],
                dst_ref=qg.at[zh, i, pl.ds(tok_row, TOK)],
                send_sem=qg_send.at[i], recv_sem=qg_recv.at[zh], device_id=(c, p), device_id_type=MESH,
            ).start()

    own_kv = kv.at[:, pl.ds(2 * BLK, BLK)]
    pltpu.make_async_copy(own_kv, own_kv, kv_recv).wait()
    for dc in (1, 2):
        pltpu.make_async_remote_copy(
            src_ref=own_kv, dst_ref=kv.at[:, pl.ds((2 - dc) * BLK, BLK)],
            send_sem=halo_send.at[dc - 1], recv_sem=halo_recv.at[dc - 1],
            device_id=(ctx_dev(dc), h), device_id_type=MESH,
        ).start()

    acc[...] = jnp.zeros_like(acc)
    pltpu.make_async_copy(doc_ref, docw.at[2], own_sem).wait()
    for dc in (1, 2):
        pltpu.make_async_copy(docw.at[2 - dc], docw.at[2 - dc], doc_recv.at[dc - 1]).wait()
    docs = jnp.concatenate([docw[0], docw[1], docw[2]], axis=1)
    lane = lax.broadcasted_iota(jnp.int32, (1, WIN), 1)
    docs = jnp.where(lane + (c - 2) * BLK >= 0, docs, -1)
    docs = jnp.broadcast_to(docs, (8, WIN))
    lane = lax.broadcasted_iota(jnp.int32, (8, WIN), 1)
    begins = jnp.where((lane == 0) | (docs != pltpu.roll(docs, 1, 1)), lane, 0)
    step = 1
    while step < WIN:
        begins = jnp.maximum(begins, jnp.where(lane >= step, pltpu.roll(begins, step, 1), 0))
        step *= 2
    for s in range(4):
        startb[s] = begins[:, 2 * BLK + s * SL : 2 * BLK + (s + 1) * SL]

    for dc in (1, 2):
        part = kv.at[:, pl.ds((2 - dc) * BLK, BLK)]
        pltpu.make_async_copy(part, part, halo_recv.at[dc - 1]).wait()

    def unit(j, carry):
        s = lax.rem(zh + jnp.where(j == 2, 3, jnp.where(j == 3, 2, j)), 4)
        pltpu.make_async_copy(qg.at[s], qg.at[s], qg_recv.at[s]).wait()
        first = pl.multiple_of(s * SL, SL)
        keys = kv[0, pl.ds(first, KEYS)]
        values = kv[1, pl.ds(first, KEYS)]
        q4 = jnp.concatenate([qg[s, 0, :, i * D : (i + 1) * D] for i in range(GRP)], axis=0)
        g4 = jnp.concatenate([qg[s, 1, :, i * D : (i + 1) * D] for i in range(GRP)], axis=0)
        start = startb[s][0:1]
        start = jnp.concatenate([start] * GRP, axis=1) - first
        scores = nt(keys, q4) * (SCALE * LOG2E)
        row = lax.broadcasted_iota(jnp.int32, (KEYS, GRP * SL), 0)
        column = lax.rem(lax.broadcasted_iota(jnp.int32, (1, GRP * SL), 1), SL) + 2 * BLK
        scores = jnp.where((row >= start) & (row <= column), scores, -jnp.inf)
        peak = jnp.max(scores, axis=0, keepdims=True)
        weights = jnp.exp2(scores - peak)
        total = jnp.sum(weights, axis=0, keepdims=True)
        weights = (weights * (1.0 / total)).astype(jnp.bfloat16)
        att = tn(values, weights).astype(jnp.bfloat16).astype(jnp.float32)
        g_t = jnp.transpose(g4.astype(jnp.float32))
        dot = jnp.sum(att * g_t, axis=0, keepdims=True)
        for i in range(GRP):
            outb[s, 0, :, i * D : (i + 1) * D] = jnp.transpose(att[:, i * D : (i + 1) * D]).astype(jnp.bfloat16)
        acc[1, pl.ds(first, KEYS)] += jnp.dot(weights, g4, preferred_element_type=jnp.float32)
        dscore = (weights.astype(jnp.float32) * (nt(values, g4) - dot)).astype(jnp.bfloat16)
        dq = tn(keys, dscore) * SCALE
        for i in range(GRP):
            outb[s, 1, :, i * D : (i + 1) * D] = jnp.transpose(dq[:, i * D : (i + 1) * D]).astype(jnp.bfloat16)
        acc[0, pl.ds(first, KEYS)] += jnp.dot(dscore, q4, preferred_element_type=jnp.float32)
        for i, dst in enumerate((att_ref, dq_ref)):
            for cc in range(2):
                piece = outb.at[s, i, pl.ds(cc * TOK, TOK)]
                there = dst.at[:, pl.ds(col_q, BLK)]

                @pl.when(2 * s + cc == h)
                def _():
                    pltpu.make_async_copy(piece, there, out_recv.at[i]).start()

                @pl.when(2 * s + cc != h)
                def _():
                    pltpu.make_async_remote_copy(
                        src_ref=piece, dst_ref=there, send_sem=out_send.at[i], recv_sem=out_recv.at[i],
                        device_id=(c, 2 * s + cc), device_id_type=MESH,
                    ).start()

        return carry

    lax.fori_loop(0, 4, unit, 0)

    for dc in (1, 2):
        rows = slice((2 - dc) * BLK, (3 - dc) * BLK)
        hsend[dc - 1, 0] = (acc[0, rows] * SCALE).astype(jnp.bfloat16)
        hsend[dc - 1, 1] = acc[1, rows].astype(jnp.bfloat16)
        pltpu.make_async_remote_copy(
            src_ref=hsend.at[dc - 1], dst_ref=hrecv.at[dc - 1],
            send_sem=part_send.at[dc - 1], recv_sem=part_recv.at[dc - 1],
            device_id=(ctx_dev(-dc), h), device_id_type=MESH,
        ).start()
    for dc in (1, 2):
        pltpu.make_async_copy(hrecv.at[dc - 1], hrecv.at[dc - 1], part_recv.at[dc - 1]).wait()
    for i in range(2):
        mine = acc[i, 2 * BLK :] * (SCALE if i == 0 else 1.0)
        osend[i] = (mine + hrecv[0, i].astype(jnp.float32) + hrecv[1, i].astype(jnp.float32)).astype(jnp.bfloat16)
    for i, dst in enumerate((dk_ref, dv_ref)):
        there = dst.at[:, pl.ds(col_k, D)]
        pltpu.make_async_copy(
            osend.at[i, pl.ds(pl.multiple_of(h * TOK, TOK), TOK)], there, grad_recv.at[i]
        ).start()
        for dz, dk in peers:
            p = head_dev(dz, dk)
            pltpu.make_async_remote_copy(
                src_ref=osend.at[i, pl.ds(pl.multiple_of(p * TOK, TOK), TOK)], dst_ref=there,
                send_sem=grad_send.at[i], recv_sem=grad_recv.at[i], device_id=(c, p), device_id_type=MESH,
            ).start()

    def drain(ref, sem):
        pltpu.make_async_copy(ref, ref, sem).wait()

    for i, dst in enumerate((att_ref, dq_ref)):
        drain(dst, out_recv.at[i])
    for i, dst in enumerate((dk_ref, dv_ref)):
        drain(dst, grad_recv.at[i])
    sent = len(peers) * TOK
    for i in range(2):
        drain(osend.at[i, pl.ds(0, sent)], grad_send.at[i])
        drain(att_ref.at[:, pl.ds(0, len(peers) * BLK)], out_send.at[i])
        drain(hsend.at[i], part_send.at[i])
        drain(own_kv, halo_send.at[i])
        drain(docw.at[i], doc_send.at[i])
    drain(kv.at[:, pl.ds(0, sent)], kv_send)
    for i in range(2):
        drain(att_ref.at[:, pl.ds(0, len(peers) * BLK)], qg_send.at[i])


def on_device(queries, stacked_keys, stacked_values, output_gradient, doc_ids):
    any_ref = pl.BlockSpec(memory_space=pl.ANY)
    dma = pltpu.SemaphoreType.DMA
    shapes = [jax.ShapeDtypeStruct(a.shape, a.dtype) for a in (queries, queries, stacked_keys, stacked_values)]
    return pl.pallas_call(
        kernel,
        out_shape=shapes,
        in_specs=[any_ref] * 5,
        out_specs=[any_ref] * 4,
        scratch_shapes=[
            pltpu.VMEM((2, WIN, D), jnp.bfloat16),
            pltpu.VMEM((4, 2, SL, BLK), jnp.bfloat16),
            pltpu.VMEM((3, 1, BLK), jnp.int32),
            pltpu.VMEM((4, 8, SL), jnp.int32),
            pltpu.VMEM((4, 2, SL, BLK), jnp.bfloat16),
            pltpu.VMEM((2, WIN, D), jnp.float32),
            pltpu.VMEM((2, 2, BLK, D), jnp.bfloat16),
            pltpu.VMEM((2, 2, BLK, D), jnp.bfloat16),
            pltpu.VMEM((2, BLK, D), jnp.bfloat16),
            dma, dma, dma((2,)), dma((4,)), dma((2,)), dma((2,)), dma((2,)), dma((2,)), dma,
            dma((2,)), dma((2,)), dma((2,)), dma((2,)), dma((2,)), dma((2,)),
        ],
        compiler_params=pltpu.CompilerParams(
            collective_id=0, has_side_effects=True, vmem_limit_bytes=48 * 2**20
        ),
    )(queries, stacked_keys, stacked_values, output_gradient, doc_ids.reshape(1, -1))


def solution(mesh):
    tokens = P(("ctx", "head"), None)
    return jax.shard_map(
        on_device, mesh=mesh, in_specs=(tokens,) * 4 + (P("ctx"),), out_specs=(tokens,) * 4, check_vma=False
    )
```

time: 237 us -> 101 us (0.43)
  the two profiles are of different devices: /device:TPU:62 before, /device:TPU:119 now
where the time goes in v1:
time: 101 us; the launch traced here: 100 us
  Pallas kernels  92.2 us (91%)
  local copies, waits for them, and re-layouts  7.46 us (7%)
    pallas_call x1, Pallas kernels, on_device(): pl.pallas_call(kernel, out_shape=shapes, in_specs=[any_ref] * 5, out_spec...  92.2 us
    unnamed x14, local copies, waits for them, and re-layouts  7.46 us

profile of v1, /device:TPU:119, one launch (start us, length us, event | category | flops | bytes accessed | tf_op | source)
XLA Modules:
  0.0 100.3 jit_solution(455621199057147027)
XLA Ops:
  0.6 0.0 copy-start
  0.6 1.0 %copy-done = bf16[64,4096]{1,0:T(8,128)(2,1)S(1)} copy-done((bf16[64,4096]{1,0:T(8,128)(2,1)S(1)}, bf16[64,4096]{1,0:T(8,128)(2,1)}, u32[]{:S(2)}) %copy-start) | copy-done | bytes 524312
  1.7 0.0 copy-start.1
  1.7 1.0 %copy-done.1 = bf16[64,4096]{1,0:T(8,128)(2,1)S(1)} copy-done((bf16[64,4096]{1,0:T(8,128)(2,1)S(1)}, bf16[64,4096]{1,0:T(8,128)(2,1)}, u32[]{:S(2)}) %copy-start.1) | copy-done | bytes 524312
  2.7 0.0 copy-start.2
  2.7 0.9 copy-done.2
  3.6 0.0 copy-start.3
  3.6 0.9 copy-done.3
  4.5 0.0 copy-start.4
  4.5 0.7 copy-done.4
  5.2 92.2 %shard_map.84 = (bf16[64,4096]{1,0:T(8,128)(2,1)S(1)}, bf16[64,4096]{1,0:T(8,128)(2,1)S(1)}, bf16[64,1024]{1,0:T(8,128)(2,1)S(1)}, bf16[64,1024]{1,0:T(8,128)(2,1)S(1)}) custom-call(bf16[64,4096]{1,0:T(8,128)(2,1)S(1)} %copy-done, bf16[64,1024]{1,0:T(8,128)(2,1)S(1)} %copy-done.2, bf16[64,1024]{1,0:T(8,128)(2,1)S(1)} %copy-done.3, ...), custom_call_target="tpu_custom_call" | custom-call | tf_op jit(solution)/shard_map/pallas_call | solution.py:220
  97.4 0.8 copy.13
  98.2 0.8 copy.14
  99.0 0.7 copy.15
  99.7 0.7 copy.16
Async XLA Ops:
  0.6 1.0 %copy-start = (bf16[64,4096]{1,0:T(8,128)(2,1)S(1)}, bf16[64,4096]{1,0:T(8,128)(2,1)}, u32[]{:S(2)}) copy-start(bf16[64,4096]{1,0:T(8,128)(2,1)} %q_ref.1) | copy-start | bytes 1572868
  1.7 1.0 %copy-start.1 = (bf16[64,4096]{1,0:T(8,128)(2,1)S(1)}, bf16[64,4096]{1,0:T(8,128)(2,1)}, u32[]{:S(2)}) copy-start(bf16[64,4096]{1,0:T(8,128)(2,1)} %g_ref.1) | copy-start | bytes 1572868
  2.7 0.9 copy-start.2
  3.6 0.9 copy-start.3
  4.5 0.7 copy-start.4

commit v2 on v1

--- a/solution.py
+++ b/solution.py
@@ -11,6 +11,7 @@
 TOK = 64
 SL = 128
 BLK = 512
+HALF = 256
 WIN = 1536
 KEYS = 1152
 GRP = 4
@@ -53,7 +54,7 @@
     col_k = pl.multiple_of(h * D, D)
     tok_row = pl.multiple_of(core * TOK, TOK)
     for i, src in enumerate((k_ref, v_ref)):
-        pltpu.make_async_copy(src.at[:, pl.ds(col_k, D)], kv.at[i, pl.ds(own_row, TOK)], kv_recv).start()
+        pltpu.make_async_copy(src.at[:, pl.ds(col_k, D)], kv.at[i, pl.ds(own_row, TOK)], kv_recv.at[i]).start()
     for i, src in enumerate((q_ref, g_ref)):
         pltpu.make_async_copy(
             src.at[:, pl.ds(col_q, BLK)], qg.at[zh, i, pl.ds(tok_row, TOK)], qg_recv.at[zh]
@@ -63,24 +64,33 @@
     barrier = pltpu.get_barrier_semaphore()
     for dz, dk in peers:
         pl.semaphore_signal(barrier, inc=1, device_id=(c, head_dev(dz, dk)), device_id_type=MESH)
-    for dc in (-2, -1, 1, 2):
+    for dc in (-1, 1):
         pl.semaphore_signal(barrier, inc=1, device_id=(ctx_dev(dc), h), device_id_type=MESH)
-    pl.semaphore_wait(barrier, len(peers) + 4)
-
-    for dz, dk in peers:
-        p = head_dev(dz, dk)
-        for i, src in enumerate((k_ref, v_ref)):
+    pl.semaphore_wait(barrier, len(peers) + 2)
+
+    for i, src in enumerate((k_ref, v_ref)):
+        for dz, dk in peers:
+            p = head_dev(dz, dk)
             pltpu.make_async_remote_copy(
                 src_ref=src.at[:, pl.ds(pl.multiple_of(p * D, D), D)],
                 dst_ref=kv.at[i, pl.ds(own_row, TOK)],
-                send_sem=kv_send, recv_sem=kv_recv, device_id=(c, p), device_id_type=MESH,
-            ).start()
-    for dc in (1, 2):
+                send_sem=kv_send, recv_sem=kv_recv.at[i], device_id=(c, p), device_id_type=MESH,
+            ).start()
+
+    after, before = (ctx_dev(1), h), (ctx_dev(-1), h)
+
+    def pass_on(src, dst, send_sem, recv_sem, to=after):
         pltpu.make_async_remote_copy(
-            src_ref=doc_ref, dst_ref=docw.at[2 - dc], send_sem=doc_send.at[dc - 1], recv_sem=doc_recv.at[dc - 1],
-            device_id=(ctx_dev(dc), h), device_id_type=MESH,
+            src_ref=src, dst_ref=dst, send_sem=send_sem, recv_sem=recv_sem, device_id=to, device_id_type=MESH
         ).start()
-    for dz, dk in peers:
+
+    def arrived(ref, sem):
+        pltpu.make_async_copy(ref, ref, sem).wait()
+
+    def chunk(i, r, block):
+        return kv.at[i, pl.ds(block * BLK + r * HALF, HALF)]
+
+    for dz, dk in peers[:5]:
         p = head_dev(dz, dk)
         for i, src in enumerate((q_ref, g_ref)):
             pltpu.make_async_remote_copy(
@@ -89,19 +99,31 @@
                 send_sem=qg_send.at[i], recv_sem=qg_recv.at[zh], device_id=(c, p), device_id_type=MESH,
             ).start()
 
-    own_kv = kv.at[:, pl.ds(2 * BLK, BLK)]
-    pltpu.make_async_copy(own_kv, own_kv, kv_recv).wait()
-    for dc in (1, 2):
-        pltpu.make_async_remote_copy(
-            src_ref=own_kv, dst_ref=kv.at[:, pl.ds((2 - dc) * BLK, BLK)],
-            send_sem=halo_send.at[dc - 1], recv_sem=halo_recv.at[dc - 1],
-            device_id=(ctx_dev(dc), h), device_id_type=MESH,
-        ).start()
+    pass_on(doc_ref, docw.at[1], doc_send.at[0], doc_recv.at[0])
+    for i in range(2):
+        arrived(kv.at[i, pl.ds(2 * BLK, BLK)], kv_recv.at[i])
+        for r in range(2):
+            pass_on(chunk(i, r, 2), chunk(i, r, 1), halo_send.at[0, i, r], halo_recv.at[0, i, r])
+
+    for dz, dk in peers[5:]:
+        p = head_dev(dz, dk)
+        for i, src in enumerate((q_ref, g_ref)):
+            pltpu.make_async_remote_copy(
+                src_ref=src.at[:, pl.ds(pl.multiple_of(p * BLK, BLK), BLK)],
+                dst_ref=qg.at[zh, i, pl.ds(tok_row, TOK)],
+                send_sem=qg_send.at[i], recv_sem=qg_recv.at[zh], device_id=(c, p), device_id_type=MESH,
+            ).start()
+
+    arrived(docw.at[1], doc_recv.at[0])
+    pass_on(docw.at[1], docw.at[0], doc_send.at[1], doc_recv.at[1])
+    for i in range(2):
+        for r in range(2):
+            arrived(chunk(i, r, 1), halo_recv.at[0, i, r])
+            pass_on(chunk(i, r, 1), chunk(i, r, 0), halo_send.at[1, i, r], halo_recv.at[1, i, r])
 
     acc[...] = jnp.zeros_like(acc)
     pltpu.make_async_copy(doc_ref, docw.at[2], own_sem).wait()
-    for dc in (1, 2):
-        pltpu.make_async_copy(docw.at[2 - dc], docw.at[2 - dc], doc_recv.at[dc - 1]).wait()
+    arrived(docw.at[0], doc_recv.at[1])
     docs = jnp.concatenate([docw[0], docw[1], docw[2]], axis=1)
     lane = lax.broadcasted_iota(jnp.int32, (1, WIN), 1)
     docs = jnp.where(lane + (c - 2) * BLK >= 0, docs, -1)
@@ -115,9 +137,9 @@
     for s in range(4):
         startb[s] = begins[:, 2 * BLK + s * SL : 2 * BLK + (s + 1) * SL]
 
-    for dc in (1, 2):
-        part = kv.at[:, pl.ds((2 - dc) * BLK, BLK)]
-        pltpu.make_async_copy(part, part, halo_recv.at[dc - 1]).wait()
+    for i in range(2):
+        for r in range(2):
+            arrived(chunk(i, r, 0), halo_recv.at[1, i, r])
 
     def unit(j, carry):
         s = lax.rem(zh + jnp.where(j == 2, 3, jnp.where(j == 3, 2, j)), 4)
@@ -168,21 +190,18 @@
 
     lax.fori_loop(0, 4, unit, 0)
 
-    for dc in (1, 2):
-        rows = slice((2 - dc) * BLK, (3 - dc) * BLK)
-        hsend[dc - 1, 0] = (acc[0, rows] * SCALE).astype(jnp.bfloat16)
-        hsend[dc - 1, 1] = acc[1, rows].astype(jnp.bfloat16)
-        pltpu.make_async_remote_copy(
-            src_ref=hsend.at[dc - 1], dst_ref=hrecv.at[dc - 1],
-            send_sem=part_send.at[dc - 1], recv_sem=part_recv.at[dc - 1],
-            device_id=(ctx_dev(-dc), h), device_id_type=MESH,
-        ).start()
-    for dc in (1, 2):
-        pltpu.make_async_copy(hrecv.at[dc - 1], hrecv.at[dc - 1], part_recv.at[dc - 1]).wait()
-    for i in range(2):
-        mine = acc[i, 2 * BLK :] * (SCALE if i == 0 else 1.0)
-        osend[i] = (mine + hrecv[0, i].astype(jnp.float32) + hrecv[1, i].astype(jnp.float32)).astype(jnp.bfloat16)
+    factors = (SCALE, 1.0)
+    for i in range(2):
+        hsend[1, i] = (acc[i, :BLK] * factors[i]).astype(jnp.bfloat16)
+        pass_on(hsend.at[1, i], hrecv.at[1, i], part_send.at[1, i], part_recv.at[1, i], before)
+    for i in range(2):
+        arrived(hrecv.at[1, i], part_recv.at[1, i])
+        hsend[0, i] = (acc[i, BLK : 2 * BLK] * factors[i] + hrecv[1, i].astype(jnp.float32)).astype(jnp.bfloat16)
+        pass_on(hsend.at[0, i], hrecv.at[0, i], part_send.at[0, i], part_recv.at[0, i], before)
     for i, dst in enumerate((dk_ref, dv_ref)):
+        arrived(hrecv.at[0, i], part_recv.at[0, i])
+        mine = acc[i, 2 * BLK :] * factors[i]
+        osend[i] = (mine + hrecv[0, i].astype(jnp.float32)).astype(jnp.bfloat16)
         there = dst.at[:, pl.ds(col_k, D)]
         pltpu.make_async_copy(
             osend.at[i, pl.ds(pl.multiple_of(h * TOK, TOK), TOK)], there, grad_recv.at[i]
@@ -194,30 +213,41 @@
                 send_sem=grad_send.at[i], recv_sem=grad_recv.at[i], device_id=(c, p), device_id_type=MESH,
             ).start()
 
-    def drain(ref, sem):
-        pltpu.make_async_copy(ref, ref, sem).wait()
-
     for i, dst in enumerate((att_ref, dq_ref)):
-        drain(dst, out_recv.at[i])
+        arrived(dst, out_recv.at[i])
     for i, dst in enumerate((dk_ref, dv_ref)):
-        drain(dst, grad_recv.at[i])
+        arrived(dst, grad_recv.at[i])
     sent = len(peers) * TOK
     for i in range(2):
-        drain(osend.at[i, pl.ds(0, sent)], grad_send.at[i])
-        drain(att_ref.at[:, pl.ds(0, len(peers) * BLK)], out_send.at[i])
-        drain(hsend.at[i], part_send.at[i])
-        drain(own_kv, halo_send.at[i])
-        drain(docw.at[i], doc_send.at[i])
-    drain(kv.at[:, pl.ds(0, sent)], kv_send)
-    for i in range(2):
-        drain(att_ref.at[:, pl.ds(0, len(peers) * BLK)], qg_send.at[i])
+        arrived(osend.at[i, pl.ds(0, sent)], grad_send.at[i])
+        arrived(att_ref.at[:, pl.ds(0, len(peers) * BLK)], out_send.at[i])
+        arrived(att_ref.at[:, pl.ds(0, len(peers) * BLK)], qg_send.at[i])
+        arrived(docw.at[i], doc_send.at[i])
+        for j in range(2):
+            arrived(hsend.at[j, i], part_send.at[j, i])
+            for r in range(2):
+                arrived(chunk(i, r, 2 - j), halo_send.at[j, i, r])
+    arrived(kv.at[:, pl.ds(0, sent)], kv_send)
+
+
+def hand_over(*refs):
+    sources, targets, stages, sems = refs[:4], refs[4:8], refs[8:12], refs[12]
+    loads = [pltpu.make_async_copy(sources[i], stages[i], sems.at[0, i]) for i in range(4)]
+    stores = [pltpu.make_async_copy(stages[i], targets[i], sems.at[1, i]) for i in range(4)]
+    for load in loads:
+        load.start()
+    for load, store in zip(loads, stores):
+        load.wait()
+        store.start()
+    for store in stores:
+        store.wait()
 
 
 def on_device(queries, stacked_keys, stacked_values, output_gradient, doc_ids):
     any_ref = pl.BlockSpec(memory_space=pl.ANY)
     dma = pltpu.SemaphoreType.DMA
     shapes = [jax.ShapeDtypeStruct(a.shape, a.dtype) for a in (queries, queries, stacked_keys, stacked_values)]
-    return pl.pallas_call(
+    results = pl.pallas_call(
         kernel,
         out_shape=shapes,
         in_specs=[any_ref] * 5,
@@ -232,13 +262,18 @@
             pltpu.VMEM((2, 2, BLK, D), jnp.bfloat16),
             pltpu.VMEM((2, 2, BLK, D), jnp.bfloat16),
             pltpu.VMEM((2, BLK, D), jnp.bfloat16),
-            dma, dma, dma((2,)), dma((4,)), dma((2,)), dma((2,)), dma((2,)), dma((2,)), dma,
-            dma((2,)), dma((2,)), dma((2,)), dma((2,)), dma((2,)), dma((2,)),
+            dma, dma((2,)), dma((2,)), dma((4,)), dma((2, 2, 2)), dma((2, 2, 2)), dma((2,)), dma((2,)), dma,
+            dma((2,)), dma((2,)), dma((2, 2)), dma((2, 2)), dma((2,)), dma((2,)),
         ],
         compiler_params=pltpu.CompilerParams(
-            collective_id=0, has_side_effects=True, vmem_limit_bytes=48 * 2**20
+            collective_id=0, has_side_effects=True, vmem_limit_bytes=60 * 2**20
         ),
     )(queries, stacked_keys, stacked_values, output_gradient, doc_ids.reshape(1, -1))
+    return pl.pallas_call(
+        hand_over, out_shape=shapes, in_specs=[any_ref] * 4, out_specs=[any_ref] * 4,
+        scratch_shapes=[pltpu.VMEM(a.shape, a.dtype) for a in shapes] + [dma((2, 4))],
+        compiler_params=pltpu.CompilerParams(vmem_limit_bytes=60 * 2**20),
+    )(*results)
 
 
 def solution(mesh):

time: 101 us -> 87.6 us (0.87)
  the two profiles are of different devices: /device:TPU:119 before, /device:TPU:57 now
where the time goes in v2:
time: 87.6 us; the launch traced here: 87.4 us
  Pallas kernels  86.8 us (99%)
    pallas_call x1, Pallas kernels, on_device(): pl.pallas_call(kernel, out_shape=shapes, in_specs=[any_ref] * 5, out_spec...  84.7 us
    pallas_call x1, Pallas kernels, on_device(): pl.pallas_call(hand_over, out_shape=shapes, in_specs=[any_ref] * 4, out_s...  2.16 us

profile of v2, /device:TPU:57, one launch (start us, length us, event | category | flops | bytes accessed | tf_op | source)
XLA Modules:
  0.0 87.4 jit_solution(3589580533189144920)
XLA Ops:
  0.6 84.7 %shard_map.84 = (bf16[64,4096]{1,0:T(8,128)(2,1)}, bf16[64,4096]{1,0:T(8,128)(2,1)}, bf16[64,1024]{1,0:T(8,128)(2,1)}, bf16[64,1024]{1,0:T(8,128)(2,1)}) custom-call(bf16[64,4096]{1,0:T(8,128)(2,1)} %q_ref.1, bf16[64,1024]{1,0:T(8,128)(2,1)} %k_ref.1, bf16[64,1024]{1,0:T(8,128)(2,1)} %v_ref.1, bf16[64,4096]{1,0:T(8,128)(2,1)} %g_ref.1, s32[1,512]{1,0:T(1,128)} %bitcast.1), custom_call_target="tpu_custom_call" | custom-call | tf_op jit(solution)/shard_map/pallas_call | solution.py:250
  85.3 2.2 %shard_map.85 = (bf16[64,4096]{1,0:T(8,128)(2,1)}, bf16[64,4096]{1,0:T(8,128)(2,1)}, bf16[64,1024]{1,0:T(8,128)(2,1)}, bf16[64,1024]{1,0:T(8,128)(2,1)}) custom-call(bf16[64,4096]{1,0:T(8,128)(2,1)} %get-tuple-element.8.refs_0_, bf16[64,4096]{1,0:T(8,128)(2,1)} %get-tuple-element.9.refs_1_, bf16[64,1024]{1,0:T(8,128)(2,1)} %get-tuple-element.10.refs_2_, ...), custom_call_target="tpu_custom_call" | custom-call | tf_op jit(solution)/shard_map/pallas_call | solution.py:272

commit v3 on v2

--- a/solution.py
+++ b/solution.py
@@ -31,9 +31,9 @@
 def kernel(
     q_ref, k_ref, v_ref, g_ref, doc_ref,
     att_ref, dq_ref, dk_ref, dv_ref,
-    kv, qg, docw, startb, outb, acc, hsend, hrecv, osend,
+    kv, qg, docw, startb, outb, acc, hsend, hrecv, osend, relay,
     kv_send, kv_recv, qg_send, qg_recv, halo_send, halo_recv, doc_send, doc_recv, own_sem,
-    out_send, out_recv, part_send, part_recv, grad_send, grad_recv,
+    out_send, out_recv, part_send, part_recv, grad_send, grad_recv, extra_send, relay_send, relay_recv,
 ):
     n_ctx = lax.axis_size("ctx")
     c = lax.axis_index("ctx")
@@ -44,8 +44,7 @@
     def head_dev(dz, dk):
         return lax.rem(zh + dz, 4) * 2 + lax.rem(core + dk, 2)
 
-    def ctx_dev(dc):
-        return lax.rem(c + dc + n_ctx, n_ctx)
+    last, seam = n_ctx - 1, n_ctx // 2
 
     peers = [(0, 1), (1, 0), (1, 1), (3, 0), (3, 1), (2, 0), (2, 1)]
 
@@ -61,12 +60,33 @@
         ).start()
     pltpu.make_async_copy(doc_ref, docw.at[2], own_sem).start()
 
+    @pl.when(c < 2)
+    def _():
+        kv[:, : 2 * BLK] = jnp.zeros((2, 2 * BLK, D), jnp.bfloat16)
+        docw[0] = jnp.full((1, BLK), -1, jnp.int32)
+        docw[1] = jnp.full((1, BLK), -1, jnp.int32)
+
+    @pl.when((c == 0) | (c == seam) | (c == last))
+    def _():
+        hrecv[...] = jnp.zeros_like(hrecv)
+
     barrier = pltpu.get_barrier_semaphore()
     for dz, dk in peers:
         pl.semaphore_signal(barrier, inc=1, device_id=(c, head_dev(dz, dk)), device_id_type=MESH)
-    for dc in (-1, 1):
-        pl.semaphore_signal(barrier, inc=1, device_id=(ctx_dev(dc), h), device_id_type=MESH)
-    pl.semaphore_wait(barrier, len(peers) + 2)
+    has_before, has_after = c >= 1, c < last
+    turning = ((c >= seam - 2) & (c <= seam)) | (c >= last - 1)
+    near = [(has_before, c - 1), (has_after, c + 1)]
+    for other in (seam - 2, seam - 1, seam, last - 1, last):
+        near.append((turning & ((c < other - 1) | (c > other + 1)), other))
+    partners = len(peers)
+    for there, other in near:
+        partners = partners + jnp.where(there, 1, 0)
+
+        @pl.when(there)
+        def _():
+            pl.semaphore_signal(barrier, inc=1, device_id=(other, h), device_id_type=MESH)
+
+    pl.semaphore_wait(barrier, partners)
 
     for i, src in enumerate((k_ref, v_ref)):
         for dz, dk in peers:
@@ -77,7 +97,7 @@
                 send_sem=kv_send, recv_sem=kv_recv.at[i], device_id=(c, p), device_id_type=MESH,
             ).start()
 
-    after, before = (ctx_dev(1), h), (ctx_dev(-1), h)
+    after, before = (c + 1, h), (c - 1, h)
 
     def pass_on(src, dst, send_sem, recv_sem, to=after):
         pltpu.make_async_remote_copy(
@@ -99,11 +119,33 @@
                 send_sem=qg_send.at[i], recv_sem=qg_recv.at[zh], device_id=(c, p), device_id_type=MESH,
             ).start()
 
-    pass_on(doc_ref, docw.at[1], doc_send.at[0], doc_recv.at[0])
+    def way(r):
+        return relay.at[0, pl.ds(r * HALF, HALF)]
+
+    @pl.when(has_after)
+    def _():
+        pass_on(doc_ref, docw.at[1], doc_send.at[0], doc_recv.at[0])
+
     for i in range(2):
         arrived(kv.at[i, pl.ds(2 * BLK, BLK)], kv_recv.at[i])
-        for r in range(2):
-            pass_on(chunk(i, r, 2), chunk(i, r, 1), halo_send.at[0, i, r], halo_recv.at[0, i, r])
+
+        @pl.when(has_after & ((c != seam - 1) | (i == 1)))
+        def _():
+            for r in range(2):
+                pass_on(chunk(i, r, 2), chunk(i, r, 1), halo_send.at[0, i, r], halo_recv.at[0, i, r])
+
+        @pl.when((c == seam - 1) & (i == 0))
+        def _():
+            for r in range(2):
+                pass_on(chunk(i, r, 2), way(r), halo_send.at[0, i, r], relay_recv.at[r], (last, h))
+
+        @pl.when(c == seam - 2)
+        def _():
+            for r in range(2):
+                if i == 0:
+                    pass_on(chunk(i, r, 2), chunk(i, r, 0), extra_send.at[i, r], halo_recv.at[1, i, r], (seam, h))
+                else:
+                    pass_on(chunk(i, r, 2), way(r), extra_send.at[i, r], relay_recv.at[r], (last - 1, h))
 
     for dz, dk in peers[5:]:
         p = head_dev(dz, dk)
@@ -114,16 +156,39 @@
                 send_sem=qg_send.at[i], recv_sem=qg_recv.at[zh], device_id=(c, p), device_id_type=MESH,
             ).start()
 
-    arrived(docw.at[1], doc_recv.at[0])
-    pass_on(docw.at[1], docw.at[0], doc_send.at[1], doc_recv.at[1])
-    for i in range(2):
-        for r in range(2):
-            arrived(chunk(i, r, 1), halo_recv.at[0, i, r])
-            pass_on(chunk(i, r, 1), chunk(i, r, 0), halo_send.at[1, i, r], halo_recv.at[1, i, r])
-
+    def turn(where, i, stage):
+        @pl.when(c == where)
+        def _():
+            for r in range(2):
+                arrived(way(r), relay_recv.at[r])
+                pass_on(way(r), chunk(i, r, 1 - stage), relay_send.at[r], halo_recv.at[stage, i, r], (seam, h))
+
+    turn(last, 0, 0)
+
+    @pl.when(has_before)
+    def _():
+        arrived(docw.at[1], doc_recv.at[0])
+
+        @pl.when(has_after)
+        def _():
+            pass_on(docw.at[1], docw.at[0], doc_send.at[1], doc_recv.at[1])
+
+        for i in range(2):
+            for r in range(2):
+                arrived(chunk(i, r, 1), halo_recv.at[0, i, r])
+
+                @pl.when(has_after & (c != seam - 1))
+                def _():
+                    pass_on(chunk(i, r, 1), chunk(i, r, 0), halo_send.at[1, i, r], halo_recv.at[1, i, r])
+
+    turn(last - 1, 1, 1)
     acc[...] = jnp.zeros_like(acc)
     pltpu.make_async_copy(doc_ref, docw.at[2], own_sem).wait()
-    arrived(docw.at[0], doc_recv.at[1])
+
+    @pl.when(c >= 2)
+    def _():
+        arrived(docw.at[0], doc_recv.at[1])
+
     docs = jnp.concatenate([docw[0], docw[1], docw[2]], axis=1)
     lane = lax.broadcasted_iota(jnp.int32, (1, WIN), 1)
     docs = jnp.where(lane + (c - 2) * BLK >= 0, docs, -1)
@@ -137,9 +202,11 @@
     for s in range(4):
         startb[s] = begins[:, 2 * BLK + s * SL : 2 * BLK + (s + 1) * SL]
 
-    for i in range(2):
-        for r in range(2):
-            arrived(chunk(i, r, 0), halo_recv.at[1, i, r])
+    @pl.when(c >= 2)
+    def _():
+        for i in range(2):
+            for r in range(2):
+                arrived(chunk(i, r, 0), halo_recv.at[1, i, r])
 
     def unit(j, carry):
         s = lax.rem(zh + jnp.where(j == 2, 3, jnp.where(j == 3, 2, j)), 4)
@@ -191,17 +258,49 @@
     lax.fori_loop(0, 4, unit, 0)
 
     factors = (SCALE, 1.0)
+
+    def give(stage, i):
+        here, there, sent = hsend.at[stage, i], hrecv.at[stage, i], part_send.at[stage, i]
+        aside = -1
+
+        side = (stage == 0) and (i == 0)
+
+        @pl.when((c >= stage + 1) & (c != (seam if side else -1)))
+        def _():
+            pass_on(here, there, sent, part_recv.at[stage, i], before)
+
+        if side:
+
+            @pl.when(c == seam)
+            def _():
+                pass_on(here, relay.at[1], sent, relay_recv.at[2], (last, h))
+
     for i in range(2):
         hsend[1, i] = (acc[i, :BLK] * factors[i]).astype(jnp.bfloat16)
-        pass_on(hsend.at[1, i], hrecv.at[1, i], part_send.at[1, i], part_recv.at[1, i], before)
+        give(1, i)
     for i in range(2):
-        arrived(hrecv.at[1, i], part_recv.at[1, i])
+
+        @pl.when(has_before & has_after)
+        def _():
+            arrived(hrecv.at[1, i], part_recv.at[1, i])
+
         hsend[0, i] = (acc[i, BLK : 2 * BLK] * factors[i] + hrecv[1, i].astype(jnp.float32)).astype(jnp.bfloat16)
-        pass_on(hsend.at[0, i], hrecv.at[0, i], part_send.at[0, i], part_recv.at[0, i], before)
+        give(0, i)
+    @pl.when(c == last)
+    def _():
+        arrived(relay.at[1], relay_recv.at[2])
+        pass_on(relay.at[1], hrecv.at[0, 0], relay_send.at[2], part_recv.at[0, 0], (seam - 1, h))
+
     for i, dst in enumerate((dk_ref, dv_ref)):
-        arrived(hrecv.at[0, i], part_recv.at[0, i])
+
+        @pl.when(has_after)
+        def _():
+            arrived(hrecv.at[0, i], part_recv.at[0, i])
+
         mine = acc[i, 2 * BLK :] * factors[i]
-        osend[i] = (mine + hrecv[0, i].astype(jnp.float32)).astype(jnp.bfloat16)
+        mine = mine + hrecv[0, i].astype(jnp.float32)
+
+        osend[i] = mine.astype(jnp.bfloat16)
         there = dst.at[:, pl.ds(col_k, D)]
         pltpu.make_async_copy(
             osend.at[i, pl.ds(pl.multiple_of(h * TOK, TOK), TOK)], there, grad_recv.at[i]
@@ -222,11 +321,40 @@
         arrived(osend.at[i, pl.ds(0, sent)], grad_send.at[i])
         arrived(att_ref.at[:, pl.ds(0, len(peers) * BLK)], out_send.at[i])
         arrived(att_ref.at[:, pl.ds(0, len(peers) * BLK)], qg_send.at[i])
-        arrived(docw.at[i], doc_send.at[i])
         for j in range(2):
-            arrived(hsend.at[j, i], part_send.at[j, i])
-            for r in range(2):
-                arrived(chunk(i, r, 2 - j), halo_send.at[j, i, r])
+
+            @pl.when(c >= j + 1)
+            def _():
+                arrived(hsend.at[j, i], part_send.at[j, i])
+
+            @pl.when(has_after if j == 0 else has_before & has_after & (c != seam - 1))
+            def _():
+                for r in range(2):
+                    arrived(chunk(i, r, 2 - j), halo_send.at[j, i, r])
+
+        @pl.when(c == seam - 2)
+        def _():
+            for r in range(2):
+                arrived(chunk(i, r, 2), extra_send.at[i, r])
+
+    @pl.when(has_after)
+    def _():
+        arrived(docw.at[1], doc_send.at[0])
+
+    @pl.when(has_before & has_after)
+    def _():
+        arrived(docw.at[1], doc_send.at[1])
+
+    @pl.when(c == last)
+    def _():
+        arrived(relay.at[1], relay_send.at[2])
+
+    @pl.when(c >= last - 1)
+    def _():
+        for r in range(2):
+            arrived(way(r), relay_send.at[r])
+
+
     arrived(kv.at[:, pl.ds(0, sent)], kv_send)
 
 
@@ -262,8 +390,10 @@
             pltpu.VMEM((2, 2, BLK, D), jnp.bfloat16),
             pltpu.VMEM((2, 2, BLK, D), jnp.bfloat16),
             pltpu.VMEM((2, BLK, D), jnp.bfloat16),
+            pltpu.VMEM((2, BLK, D), jnp.bfloat16),
             dma, dma((2,)), dma((2,)), dma((4,)), dma((2, 2, 2)), dma((2, 2, 2)), dma((2,)), dma((2,)), dma,
             dma((2,)), dma((2,)), dma((2, 2)), dma((2, 2)), dma((2,)), dma((2,)),
+            dma((2, 2)), dma((3,)), dma((3,)),
         ],
         compiler_params=pltpu.CompilerParams(
             collective_id=0, has_side_effects=True, vmem_limit_bytes=60 * 2**20

time: 87.6 us -> 83.7 us (0.955)
  the two profiles are of different devices: /device:TPU:57 before, /device:TPU:121 now
where the time goes in v3:
time: 83.7 us; the launch traced here: 83.5 us
  Pallas kernels  82.9 us (99%)
    pallas_call x1, Pallas kernels, on_device(): pl.pallas_call(kernel, out_shape=shapes, in_specs=[any_ref] * 5, out_spec...  80.7 us
    pallas_call x1, Pallas kernels, on_device(): pl.pallas_call(hand_over, out_shape=shapes, in_specs=[any_ref] * 4, out_s...  2.16 us

profile of v3, /device:TPU:121, one launch (start us, length us, event | category | flops | bytes accessed | tf_op | source)
XLA Modules:
  0.0 83.5 jit_solution(14498499016638304842)
XLA Ops:
  0.6 80.7 %shard_map.84 = (bf16[64,4096]{1,0:T(8,128)(2,1)}, bf16[64,4096]{1,0:T(8,128)(2,1)}, bf16[64,1024]{1,0:T(8,128)(2,1)}, bf16[64,1024]{1,0:T(8,128)(2,1)}) custom-call(bf16[64,4096]{1,0:T(8,128)(2,1)} %q_ref.1, bf16[64,1024]{1,0:T(8,128)(2,1)} %k_ref.1, bf16[64,1024]{1,0:T(8,128)(2,1)} %v_ref.1, bf16[64,4096]{1,0:T(8,128)(2,1)} %g_ref.1, s32[1,512]{1,0:T(1,128)} %bitcast.1), custom_call_target="tpu_custom_call" | custom-call | tf_op jit(solution)/shard_map/pallas_call | solution.py:378
  81.4 2.2 %shard_map.85 = (bf16[64,4096]{1,0:T(8,128)(2,1)}, bf16[64,4096]{1,0:T(8,128)(2,1)}, bf16[64,1024]{1,0:T(8,128)(2,1)}, bf16[64,1024]{1,0:T(8,128)(2,1)}) custom-call(bf16[64,4096]{1,0:T(8,128)(2,1)} %get-tuple-element.8.refs_0_, bf16[64,4096]{1,0:T(8,128)(2,1)} %get-tuple-element.9.refs_1_, bf16[64,1024]{1,0:T(8,128)(2,1)} %get-tuple-element.10.refs_2_, ...), custom_call_target="tpu_custom_call" | custom-call | tf_op jit(solution)/shard_map/pallas_call | solution.py:402

commit v4 on v3

--- a/solution.py
+++ b/solution.py
@@ -31,9 +31,9 @@
 def kernel(
     q_ref, k_ref, v_ref, g_ref, doc_ref,
     att_ref, dq_ref, dk_ref, dv_ref,
-    kv, qg, docw, startb, outb, acc, hsend, hrecv, osend, relay,
+    kv, qg, docw, startb, outb, acc, hsend, hrecv, osend, relay, probs,
     kv_send, kv_recv, qg_send, qg_recv, halo_send, halo_recv, doc_send, doc_recv, own_sem,
-    out_send, out_recv, part_send, part_recv, grad_send, grad_recv, extra_send, relay_send, relay_recv,
+    out_send, out_recv, part_send, part_recv, grad_send, grad_recv, extra_send, relay_send, relay_recv, go_sem,
 ):
     n_ctx = lax.axis_size("ctx")
     c = lax.axis_index("ctx")
@@ -66,7 +66,7 @@
         docw[0] = jnp.full((1, BLK), -1, jnp.int32)
         docw[1] = jnp.full((1, BLK), -1, jnp.int32)
 
-    @pl.when((c == 0) | (c == seam) | (c == last))
+    @pl.when((c == 0) | (c == seam - 1) | (c == last))
     def _():
         hrecv[...] = jnp.zeros_like(hrecv)
 
@@ -202,95 +202,121 @@
     for s in range(4):
         startb[s] = begins[:, 2 * BLK + s * SL : 2 * BLK + (s + 1) * SL]
 
-    @pl.when(c >= 2)
-    def _():
-        for i in range(2):
+    def earliest(i):
+        @pl.when(c >= 2)
+        def _():
             for r in range(2):
                 arrived(chunk(i, r, 0), halo_recv.at[1, i, r])
 
-    def unit(j, carry):
-        s = lax.rem(zh + jnp.where(j == 2, 3, jnp.where(j == 3, 2, j)), 4)
-        pltpu.make_async_copy(qg.at[s], qg.at[s], qg_recv.at[s]).wait()
+    def stacked(s, which):
+        return jnp.concatenate([qg[s, which, :, i * D : (i + 1) * D] for i in range(GRP)], axis=0)
+
+    def weigh(s):
+        arrived(qg.at[s], qg_recv.at[s])
         first = pl.multiple_of(s * SL, SL)
-        keys = kv[0, pl.ds(first, KEYS)]
-        values = kv[1, pl.ds(first, KEYS)]
-        q4 = jnp.concatenate([qg[s, 0, :, i * D : (i + 1) * D] for i in range(GRP)], axis=0)
-        g4 = jnp.concatenate([qg[s, 1, :, i * D : (i + 1) * D] for i in range(GRP)], axis=0)
+        q4 = stacked(s, 0)
         start = startb[s][0:1]
         start = jnp.concatenate([start] * GRP, axis=1) - first
-        scores = nt(keys, q4) * (SCALE * LOG2E)
-        row = lax.broadcasted_iota(jnp.int32, (KEYS, GRP * SL), 0)
-        column = lax.rem(lax.broadcasted_iota(jnp.int32, (1, GRP * SL), 1), SL) + 2 * BLK
-        scores = jnp.where((row >= start) & (row <= column), scores, -jnp.inf)
-        peak = jnp.max(scores, axis=0, keepdims=True)
-        weights = jnp.exp2(scores - peak)
-        total = jnp.sum(weights, axis=0, keepdims=True)
-        weights = (weights * (1.0 / total)).astype(jnp.bfloat16)
+        early, late = 2 * BLK, SL
+        row = lax.broadcasted_iota(jnp.int32, (early, GRP * SL), 0)
+        far = nt(kv[0, pl.ds(first, early)], q4) * (SCALE * LOG2E)
+        far = jnp.where(row >= start, far, -jnp.inf)
+        row = lax.broadcasted_iota(jnp.int32, (late, GRP * SL), 0)
+        column = lax.rem(lax.broadcasted_iota(jnp.int32, (1, GRP * SL), 1), SL)
+        close = nt(kv[0, pl.ds(pl.multiple_of(first + early, SL), late)], q4) * (SCALE * LOG2E)
+        close = jnp.where((row >= start - early) & (row <= column), close, -jnp.inf)
+        peak = jnp.maximum(jnp.max(far, axis=0, keepdims=True), jnp.max(close, axis=0, keepdims=True))
+        far, close = jnp.exp2(far - peak), jnp.exp2(close - peak)
+        part = 1.0 / (jnp.sum(far, axis=0, keepdims=True) + jnp.sum(close, axis=0, keepdims=True))
+        probs[s, :early] = (far * part).astype(jnp.bfloat16)
+        probs[s, early:] = (close * part).astype(jnp.bfloat16)
+
+    def send_back(s, i):
+        dst = (att_ref, dq_ref)[i]
+        for cc in range(2):
+            piece = outb.at[s, i, pl.ds(cc * TOK, TOK)]
+            there = dst.at[:, pl.ds(col_q, BLK)]
+
+            @pl.when(2 * s + cc == h)
+            def _():
+                pltpu.make_async_copy(piece, there, out_recv.at[i]).start()
+
+            @pl.when(2 * s + cc != h)
+            def _():
+                pltpu.make_async_remote_copy(
+                    src_ref=piece, dst_ref=there, send_sem=out_send.at[i], recv_sem=out_recv.at[i],
+                    device_id=(c, 2 * s + cc), device_id_type=MESH,
+                ).start()
+
+    def weigh_near(j, carry):
+        weigh(lax.rem(zh + jnp.where(j == 2, 3, j), 4))
+        return carry
+
+    def unit(j, carry):
+        s = lax.rem(zh + jnp.where(j == 0, 1, jnp.where(j == 1, 3, jnp.where(j == 2, 0, 2))), 4)
+
+        @pl.when(j == 3)
+        def _():
+            weigh(s)
+
+        first = pl.multiple_of(s * SL, SL)
+        values = kv[1, pl.ds(first, KEYS)]
+        weights = probs[s]
+        g4 = stacked(s, 1)
         att = tn(values, weights).astype(jnp.bfloat16).astype(jnp.float32)
-        g_t = jnp.transpose(g4.astype(jnp.float32))
-        dot = jnp.sum(att * g_t, axis=0, keepdims=True)
         for i in range(GRP):
             outb[s, 0, :, i * D : (i + 1) * D] = jnp.transpose(att[:, i * D : (i + 1) * D]).astype(jnp.bfloat16)
-        acc[1, pl.ds(first, KEYS)] += jnp.dot(weights, g4, preferred_element_type=jnp.float32)
+        send_back(s, 0)
+        dot = jnp.sum(att * jnp.transpose(g4.astype(jnp.float32)), axis=0, keepdims=True)
         dscore = (weights.astype(jnp.float32) * (nt(values, g4) - dot)).astype(jnp.bfloat16)
-        dq = tn(keys, dscore) * SCALE
+        dq = tn(kv[0, pl.ds(first, KEYS)], dscore) * SCALE
         for i in range(GRP):
             outb[s, 1, :, i * D : (i + 1) * D] = jnp.transpose(dq[:, i * D : (i + 1) * D]).astype(jnp.bfloat16)
-        acc[0, pl.ds(first, KEYS)] += jnp.dot(dscore, q4, preferred_element_type=jnp.float32)
-        for i, dst in enumerate((att_ref, dq_ref)):
-            for cc in range(2):
-                piece = outb.at[s, i, pl.ds(cc * TOK, TOK)]
-                there = dst.at[:, pl.ds(col_q, BLK)]
-
-                @pl.when(2 * s + cc == h)
-                def _():
-                    pltpu.make_async_copy(piece, there, out_recv.at[i]).start()
-
-                @pl.when(2 * s + cc != h)
-                def _():
-                    pltpu.make_async_remote_copy(
-                        src_ref=piece, dst_ref=there, send_sem=out_send.at[i], recv_sem=out_recv.at[i],
-                        device_id=(c, 2 * s + cc), device_id_type=MESH,
-                    ).start()
-
+        send_back(s, 1)
+        acc[0, pl.ds(first, KEYS)] += jnp.dot(dscore, stacked(s, 0), preferred_element_type=jnp.float32)
+        acc[1, pl.ds(first, KEYS)] += jnp.dot(weights, g4, preferred_element_type=jnp.float32)
         return carry
 
+    earliest(0)
+    lax.fori_loop(0, 3, weigh_near, 0)
+    earliest(1)
+
+    @pl.when(c == 1)
+    def _():
+        pl.semaphore_signal(go_sem, inc=1, device_id=(0, h), device_id_type=MESH)
+
+    @pl.when(c == 0)
+    def _():
+        pl.semaphore_wait(go_sem, 1)
+
     lax.fori_loop(0, 4, unit, 0)
 
     factors = (SCALE, 1.0)
 
     def give(stage, i):
-        here, there, sent = hsend.at[stage, i], hrecv.at[stage, i], part_send.at[stage, i]
-        aside = -1
-
-        side = (stage == 0) and (i == 0)
-
-        @pl.when((c >= stage + 1) & (c != (seam if side else -1)))
-        def _():
-            pass_on(here, there, sent, part_recv.at[stage, i], before)
-
-        if side:
+        here, sent = hsend.at[stage, i], part_send.at[stage, i]
+
+        @pl.when((c >= stage + 1) & (c != (seam if stage == 1 else -1)))
+        def _():
+            pass_on(here, hrecv.at[stage, i], sent, part_recv.at[stage, i], before)
+
+        if stage == 1:
 
             @pl.when(c == seam)
             def _():
-                pass_on(here, relay.at[1], sent, relay_recv.at[2], (last, h))
+                pass_on(here, relay.at[i], sent, relay_recv.at[i], (seam - 2, h))
 
     for i in range(2):
         hsend[1, i] = (acc[i, :BLK] * factors[i]).astype(jnp.bfloat16)
         give(1, i)
     for i in range(2):
 
-        @pl.when(has_before & has_after)
+        @pl.when(has_before & has_after & (c != seam - 1))
         def _():
             arrived(hrecv.at[1, i], part_recv.at[1, i])
 
         hsend[0, i] = (acc[i, BLK : 2 * BLK] * factors[i] + hrecv[1, i].astype(jnp.float32)).astype(jnp.bfloat16)
         give(0, i)
-    @pl.when(c == last)
-    def _():
-        arrived(relay.at[1], relay_recv.at[2])
-        pass_on(relay.at[1], hrecv.at[0, 0], relay_send.at[2], part_recv.at[0, 0], (seam - 1, h))
-
     for i, dst in enumerate((dk_ref, dv_ref)):
 
         @pl.when(has_after)
@@ -300,7 +326,16 @@
         mine = acc[i, 2 * BLK :] * factors[i]
         mine = mine + hrecv[0, i].astype(jnp.float32)
 
-        osend[i] = mine.astype(jnp.bfloat16)
+
+        @pl.when(c != seam - 2)
+        def _():
+            osend[i] = mine.astype(jnp.bfloat16)
+
+        @pl.when(c == seam - 2)
+        def _():
+            arrived(relay.at[i], relay_recv.at[i])
+            osend[i] = (mine + relay[i].astype(jnp.float32)).astype(jnp.bfloat16)
+
         there = dst.at[:, pl.ds(col_k, D)]
         pltpu.make_async_copy(
             osend.at[i, pl.ds(pl.multiple_of(h * TOK, TOK), TOK)], there, grad_recv.at[i]
@@ -344,10 +379,6 @@
     @pl.when(has_before & has_after)
     def _():
         arrived(docw.at[1], doc_send.at[1])
-
-    @pl.when(c == last)
-    def _():
-        arrived(relay.at[1], relay_send.at[2])
 
     @pl.when(c >= last - 1)
     def _():
@@ -391,9 +422,10 @@
             pltpu.VMEM((2, 2, BLK, D), jnp.bfloat16),
             pltpu.VMEM((2, BLK, D), jnp.bfloat16),
             pltpu.VMEM((2, BLK, D), jnp.bfloat16),
+            pltpu.VMEM((4, KEYS, GRP * SL), jnp.bfloat16),
             dma, dma((2,)), dma((2,)), dma((4,)), dma((2, 2, 2)), dma((2, 2, 2)), dma((2,)), dma((2,)), dma,
             dma((2,)), dma((2,)), dma((2, 2)), dma((2, 2)), dma((2,)), dma((2,)),
-            dma((2, 2)), dma((3,)), dma((3,)),
+            dma((2, 2)), dma((3,)), dma((3,)), pltpu.SemaphoreType.REGULAR,
         ],
         compiler_params=pltpu.CompilerParams(
             collective_id=0, has_side_effects=True, vmem_limit_bytes=60 * 2**20

time: 83.7 us -> 81.9 us (0.978)
  Pallas kernels: 82.9 us -> 81.1 us
    pallas_call x1, Pallas kernels: 80.7 us -> 79 us  [on_device(): pl.pallas_call(kernel, out_shape=shapes, in_specs=[any_ref] * 5, out_spec...]
where the time goes in v4:
time: 81.9 us; the launch traced here: 81.7 us
  Pallas kernels  81.1 us (99%)
    pallas_call x1, Pallas kernels, on_device(): pl.pallas_call(kernel, out_shape=shapes, in_specs=[any_ref] * 5, out_spec...  79 us
    pallas_call x1, Pallas kernels, on_device(): pl.pallas_call(hand_over, out_shape=shapes, in_specs=[any_ref] * 4, out_s...  2.16 us

profile of v4, /device:TPU:121, one launch (start us, length us, event | category | flops | bytes accessed | tf_op | source)
XLA Modules:
  0.0 81.7 jit_solution(3550773114842524860)
XLA Ops:
  0.6 79.0 %shard_map.84 = (bf16[64,4096]{1,0:T(8,128)(2,1)}, bf16[64,4096]{1,0:T(8,128)(2,1)}, bf16[64,1024]{1,0:T(8,128)(2,1)}, bf16[64,1024]{1,0:T(8,128)(2,1)}) custom-call(bf16[64,4096]{1,0:T(8,128)(2,1)} %q_ref.1, bf16[64,1024]{1,0:T(8,128)(2,1)} %k_ref.1, bf16[64,1024]{1,0:T(8,128)(2,1)} %v_ref.1, bf16[64,4096]{1,0:T(8,128)(2,1)} %g_ref.1, s32[1,512]{1,0:T(1,128)} %bitcast.1), custom_call_target="tpu_custom_call" | custom-call | tf_op jit(solution)/shard_map/pallas_call | solution.py:409
  79.6 2.2 %shard_map.85 = (bf16[64,4096]{1,0:T(8,128)(2,1)}, bf16[64,4096]{1,0:T(8,128)(2,1)}, bf16[64,1024]{1,0:T(8,128)(2,1)}, bf16[64,1024]{1,0:T(8,128)(2,1)}) custom-call(bf16[64,4096]{1,0:T(8,128)(2,1)} %get-tuple-element.8.refs_0_, bf16[64,4096]{1,0:T(8,128)(2,1)} %get-tuple-element.9.refs_1_, bf16[64,1024]{1,0:T(8,128)(2,1)} %get-tuple-element.10.refs_2_, ...), custom_call_target="tpu_custom_call" | custom-call | tf_op jit(solution)/shard_map/pallas_call | solution.py:434

commit v5 on v4

--- a/solution.py
+++ b/solution.py
@@ -390,16 +390,12 @@
 
 
 def hand_over(*refs):
-    sources, targets, stages, sems = refs[:4], refs[4:8], refs[8:12], refs[12]
-    loads = [pltpu.make_async_copy(sources[i], stages[i], sems.at[0, i]) for i in range(4)]
-    stores = [pltpu.make_async_copy(stages[i], targets[i], sems.at[1, i]) for i in range(4)]
-    for load in loads:
-        load.start()
-    for load, store in zip(loads, stores):
-        load.wait()
-        store.start()
-    for store in stores:
-        store.wait()
+    sources, targets, sems = refs[:4], refs[4:8], refs[8]
+    copies = [pltpu.make_async_copy(sources[i], targets[i], sems.at[i]) for i in range(4)]
+    for copy in copies:
+        copy.start()
+    for copy in copies:
+        copy.wait()
 
 
 def on_device(queries, stacked_keys, stacked_values, output_gradient, doc_ids):
@@ -408,7 +404,7 @@
     shapes = [jax.ShapeDtypeStruct(a.shape, a.dtype) for a in (queries, queries, stacked_keys, stacked_values)]
     results = pl.pallas_call(
         kernel,
-        out_shape=shapes,
+        out_shape=[pltpu.VMEM(a.shape, a.dtype) for a in shapes],
         in_specs=[any_ref] * 5,
         out_specs=[any_ref] * 4,
         scratch_shapes=[
@@ -433,8 +429,8 @@
     )(queries, stacked_keys, stacked_values, output_gradient, doc_ids.reshape(1, -1))
     return pl.pallas_call(
         hand_over, out_shape=shapes, in_specs=[any_ref] * 4, out_specs=[any_ref] * 4,
-        scratch_shapes=[pltpu.VMEM(a.shape, a.dtype) for a in shapes] + [dma((2, 4))],
-        compiler_params=pltpu.CompilerParams(vmem_limit_bytes=60 * 2**20),
+        scratch_shapes=[dma((4,))],
+        compiler_params=pltpu.CompilerParams(vmem_limit_bytes=16 * 2**20),
     )(*results)
 
 

time: 81.9 us -> 80.7 us (0.985)
  Pallas kernels: 81.1 us -> 79.9 us
    pallas_call x1, Pallas kernels: 2.16 us -> 1.08 us  [on_device(): pl.pallas_call(hand_over, out_shape=shapes, in_specs=[any_ref] * 4, out_s...]
where the time goes in v5:
time: 80.7 us; the launch traced here: 80.5 us
  Pallas kernels  79.9 us (99%)
    pallas_call x1, Pallas kernels, on_device(): pl.pallas_call(kernel, out_shape=[pltpu.VMEM(a.shape, a.dtype) for a in s...  78.8 us

profile of v5, /device:TPU:121, one launch (start us, length us, event | category | flops | bytes accessed | tf_op | source)
XLA Modules:
  0.0 80.5 jit_solution(2215538890200796790)
XLA Ops:
  0.6 78.8 %shard_map.84 = (bf16[64,4096]{1,0:T(8,128)(2,1)S(1)}, bf16[64,4096]{1,0:T(8,128)(2,1)S(1)}, bf16[64,1024]{1,0:T(8,128)(2,1)S(1)}, bf16[64,1024]{1,0:T(8,128)(2,1)S(1)}) custom-call(bf16[64,4096]{1,0:T(8,128)(2,1)} %q_ref.1, bf16[64,1024]{1,0:T(8,128)(2,1)} %k_ref.1, bf16[64,1024]{1,0:T(8,128)(2,1)} %v_ref.1, bf16[64,4096]{1,0:T(8,128)(2,1)} %g_ref.1, ...), custom_call_target="tpu_custom_call" | custom-call | tf_op jit(solution)/shard_map/pallas_call | solution.py:405
  79.5 1.1 %shard_map.85 = (bf16[64,4096]{1,0:T(8,128)(2,1)}, bf16[64,4096]{1,0:T(8,128)(2,1)}, bf16[64,1024]{1,0:T(8,128)(2,1)}, bf16[64,1024]{1,0:T(8,128)(2,1)}) custom-call(bf16[64,4096]{1,0:T(8,128)(2,1)S(1)} %get-tuple-element.8.refs_0_, bf16[64,4096]{1,0:T(8,128)(2,1)S(1)} %get-tuple-element.9.refs_1_, bf16[64,1024]{1,0:T(8,128)(2,1)S(1)} %get-tuple-element.10.refs_2_, ...), custom_call_target="tpu_custom_call" | custom-call | tf_op jit(solution)/shard_map/pallas_call | solution.py:430

commit v6 on v5

--- a/solution.py
+++ b/solution.py
@@ -52,13 +52,6 @@
     col_q = pl.multiple_of(h * BLK, BLK)
     col_k = pl.multiple_of(h * D, D)
     tok_row = pl.multiple_of(core * TOK, TOK)
-    for i, src in enumerate((k_ref, v_ref)):
-        pltpu.make_async_copy(src.at[:, pl.ds(col_k, D)], kv.at[i, pl.ds(own_row, TOK)], kv_recv.at[i]).start()
-    for i, src in enumerate((q_ref, g_ref)):
-        pltpu.make_async_copy(
-            src.at[:, pl.ds(col_q, BLK)], qg.at[zh, i, pl.ds(tok_row, TOK)], qg_recv.at[zh]
-        ).start()
-    pltpu.make_async_copy(doc_ref, docw.at[2], own_sem).start()
 
     @pl.when(c < 2)
     def _():
@@ -86,10 +79,17 @@
         def _():
             pl.semaphore_signal(barrier, inc=1, device_id=(other, h), device_id_type=MESH)
 
+    for i, src in enumerate((k_ref, v_ref)):
+        pltpu.make_async_copy(src.at[:, pl.ds(col_k, D)], kv.at[i, pl.ds(own_row, TOK)], kv_recv.at[i]).start()
+    for i, src in enumerate((q_ref, g_ref)):
+        pltpu.make_async_copy(
+            src.at[:, pl.ds(col_q, BLK)], qg.at[zh, i, pl.ds(tok_row, TOK)], qg_recv.at[zh]
+        ).start()
+    pltpu.make_async_copy(doc_ref, docw.at[2], own_sem).start()
     pl.semaphore_wait(barrier, partners)
 
     for i, src in enumerate((k_ref, v_ref)):
-        for dz, dk in peers:
+        for dz, dk in reversed(peers):
             p = head_dev(dz, dk)
             pltpu.make_async_remote_copy(
                 src_ref=src.at[:, pl.ds(pl.multiple_of(p * D, D), D)],
@@ -340,7 +340,7 @@
         pltpu.make_async_copy(
             osend.at[i, pl.ds(pl.multiple_of(h * TOK, TOK), TOK)], there, grad_recv.at[i]
         ).start()
-        for dz, dk in peers:
+        for dz, dk in reversed(peers):
             p = head_dev(dz, dk)
             pltpu.make_async_remote_copy(
                 src_ref=osend.at[i, pl.ds(pl.multiple_of(p * TOK, TOK), TOK)], dst_ref=there,

time: 80.7 us -> 85.4 us (1.058)
  Pallas kernels: 79.9 us -> 84.3 us
    pallas_call x1, Pallas kernels: 78.8 us -> 83.3 us  [on_device(): pl.pallas_call(kernel, out_shape=[pltpu.VMEM(a.shape, a.dtype) for a in s...]
where the time goes in v6:
time: 85.4 us; the launch traced here: 85 us
  Pallas kernels  84.3 us (99%)
    pallas_call x1, Pallas kernels, on_device(): pl.pallas_call(kernel, out_shape=[pltpu.VMEM(a.shape, a.dtype) for a in s...  83.3 us

profile of v6, /device:TPU:121, one launch (start us, length us, event | category | flops | bytes accessed | tf_op | source)
XLA Modules:
  0.0 85.0 jit_solution(16213247505768580791)
XLA Ops:
  0.6 83.3 %shard_map.84 = (bf16[64,4096]{1,0:T(8,128)(2,1)S(1)}, bf16[64,4096]{1,0:T(8,128)(2,1)S(1)}, bf16[64,1024]{1,0:T(8,128)(2,1)S(1)}, bf16[64,1024]{1,0:T(8,128)(2,1)S(1)}) custom-call(bf16[64,4096]{1,0:T(8,128)(2,1)} %q_ref.1, bf16[64,1024]{1,0:T(8,128)(2,1)} %k_ref.1, bf16[64,1024]{1,0:T(8,128)(2,1)} %v_ref.1, bf16[64,4096]{1,0:T(8,128)(2,1)} %g_ref.1, ...), custom_call_target="tpu_custom_call" | custom-call | tf_op jit(solution)/shard_map/pallas_call | solution.py:405
  83.9 1.1 %shard_map.85 = (bf16[64,4096]{1,0:T(8,128)(2,1)}, bf16[64,4096]{1,0:T(8,128)(2,1)}, bf16[64,1024]{1,0:T(8,128)(2,1)}, bf16[64,1024]{1,0:T(8,128)(2,1)}) custom-call(bf16[64,4096]{1,0:T(8,128)(2,1)S(1)} %get-tuple-element.8.refs_0_, bf16[64,4096]{1,0:T(8,128)(2,1)S(1)} %get-tuple-element.9.refs_1_, bf16[64,1024]{1,0:T(8,128)(2,1)S(1)} %get-tuple-element.10.refs_2_, ...), custom_call_target="tpu_custom_call" | custom-call | tf_op jit(solution)/shard_map/pallas_call | solution.py:430
